TPU v7x, 32 devices: a whole 2x2x4 slice. The times are simulated.
32 devices in a mesh: dom: 16 (over z, x, core), head: 2 (over y).
Axes of the slice: x: 2, y: 2, z: 4, core: 2. Of those that a mesh axis runs over, the one named last changes fastest.
Arguments:
- node_feats: bfloat16 [4096, 512], P(('dom', 'head')), may hold values from -6 to 6
- norm_gain: float32 [512], replicated, may hold values from 0.25 to 1.75
- w_qkv: bfloat16 [512, 1536], P(None, 'head'), may hold values from -1 to 1
- w_out: bfloat16 [512, 512], replicated, may hold values from -0.25 to 0.25
- rand_feat: float32 [8, 64, 256], P('head'), may hold values from -6 to 6
- temper: float32 [8], P('head'), may hold values from 1 to 6
- edge_src: int32 [32, 6], P('dom'), may hold values from 0 to 31, as said below
- edge_count: int32 [32], P('dom'), may hold values from 1 to 6, as said below
- block_fill: int32 [32], replicated, may hold values from 32 to 128, as said below
Outputs:
- update: bfloat16 [4096, 512], P(('dom', 'head'))
Inputs may be any that keep to these rules, and one draw needn't show every extreme that they name: `edge_src`: destination block b lies in partition p = b // 2; each of its source blocks lies in partition p - 1, p or p + 1; slot 0 holds b itself, and slots at or beyond edge_count[b] hold b. `edge_count`: every block of some partition uses all 6 slots. `block_fill`: block 0 is full.
All inputs are finite; a program needn't handle non-finite values.
Results may differ from a plain program's by a relative error of at most 0.012.
The roundings to bfloat16 on the way count: a program that leaves them out, or rounds other values in their place, can miss the bound.
Values may be sent and summed in bfloat16 or wider, within the bound.
No kernel may reach another device: no remote copies, remote signals or barrier semaphores. Data moves between devices by JAX's collectives and lax.ppermute only.
A program may use at most 64 MiB of HBM per device.

v0:
```python
import functools
import math

import jax
import jax.numpy as jnp
from jax import lax
from jax.experimental import pallas as pl
from jax.experimental.pallas import tpu as pltpu
from jax.sharding import PartitionSpec as P

BLK = 128
NEG = -1e30
LOG2E = 1.4426950408889634
VM = pl.BlockSpec(memory_space=pltpu.VMEM)
SM = pl.BlockSpec(memory_space=pltpu.SMEM)
HB = pl.BlockSpec(memory_space=pltpu.HBM)
F32 = jnp.float32
BF16 = jnp.bfloat16
EXTRA = 8


def norm_rows(rows, gain):
    wide = rows.astype(F32)
    centred = wide - jnp.mean(wide, axis=-1, keepdims=True)
    spread = jnp.mean(centred * centred, axis=-1, keepdims=True)
    return (centred * lax.rsqrt(spread + 1e-05) * gain).astype(BF16)


def dot_nn(a, b):
    return lax.dot_general(a, b, (((1,), (0,)), ((), ())), preferred_element_type=F32)


def dot_nt(a, b):
    return lax.dot_general(a, b, (((1,), (1,)), ((), ())), preferred_element_type=F32)


def dot_tn(a, b):
    return lax.dot_general(a, b, (((0,), (0,)), ((), ())), preferred_element_type=F32)


def row_scale(temper, head_dim):
    return jnp.sqrt(jnp.full((1, 1), temper, F32)) * head_dim ** (-0.25)


def split_directions(directions, scale):
    scaled = directions * (scale * LOG2E)
    first = scaled.astype(BF16)
    second = (scaled - first.astype(F32)).astype(BF16)
    return jnp.concatenate([first, second], axis=0)


def features(u, both, factor, hidden=0.0):
    lifted = dot_nn(jnp.concatenate([u, u], axis=1), both)
    wide = u.astype(F32)
    square = jnp.sum(wide * wide, axis=-1, keepdims=True)
    shift = square * factor + (0.5 * math.log2(both.shape[1]) + hidden)
    return jnp.exp2(lifted - shift)


def hide(fills):
    row = lax.broadcasted_iota(jnp.int32, (BLK, 1), 0)
    return jnp.concatenate([jnp.where(row < fill, 0.0, -NEG) for fill in fills], axis=0)


def head_sums(h, out, both, factor, hidden):
    head_dim = both.shape[1] // 2
    at = h * 3 * head_dim
    key = out[:, at + head_dim : at + 2 * head_dim]
    value = out[:, at + 2 * head_dim : at + 3 * head_dim]
    phi = features(key, both[h], factor, hidden)
    return dot_tn(value, phi.astype(BF16)), jnp.sum(phi, axis=0, keepdims=True)


def head_at(heads, where, h):
    if heads % 2:
        return h
    return lax.rem(h + lax.rem(where[0], 2) * (heads // 2), heads)


def own_kernel(
    heads, groups, where, temper_in, fill_in, src_in, used_in, feats_in, gain_in, w_in,
    directions_in, w_out_in, qkv, sums, gain, w, both, w_out, factors, hidden, bias, feats,
    directions, temper, fill, src, used, sems
):
    width = w_out.shape[0] // groups
    head_dim, count = directions.shape[1:]
    cols = 3 * head_dim
    turns = 2 if heads % 2 == 0 else 1
    each = heads // turns
    copies = []

    def copy(source, target):
        copies.append(pltpu.make_async_copy(source, target, sems.at[len(copies)]))
        copies[-1].start()
        return copies[-1]

    on_feats = [copy(feats_in, feats), copy(gain_in, gain)]
    on_w, on_rest = [], [
        copy(temper_in, temper), copy(fill_in, fill), copy(src_in, src), copy(used_in, used)
    ]
    for t in range(turns):
        at = head_at(heads, where, t * each)
        on_w.append(
            copy(
                w_in.at[:, pl.ds(pl.multiple_of(at * cols, each * cols), each * cols)],
                w.at[:, pl.ds(t * each * cols, each * cols)],
            )
        )
        on_rest.append(
            copy(directions_in.at[pl.ds(at, each)], directions.at[pl.ds(t * each, each)])
        )
    on_out = []
    for k in range(groups):
        source = lax.rem(where[1] + groups - k, groups) * width
        for t in range(turns):
            size = each * head_dim
            at = pl.multiple_of(source + head_at(heads, where, t * each) * head_dim, size)
            on_out.append(
                copy(
                    w_out_in.at[pl.ds(at, size), :],
                    w_out.at[pl.ds(k * width + t * size, size), :],
                )
            )
    for item in on_feats:
        item.wait()
    normed = norm_rows(feats[...], gain[...])
    for item in on_w:
        item.wait()
    out = dot_nn(normed, w[...]).astype(BF16)
    qkv[...] = out
    for item in on_rest:
        item.wait()
    mine = feats.shape[0] // BLK
    fills = [
        fill[(where[0] * groups + lax.rem(where[1] + k, groups)) * mine + t]
        for k in range(groups)
        for t in range(mine)
    ]
    hidden[...] = hide(fills[mine:])
    own_hidden = hide(fills[:mine])
    totals = []
    for h in range(heads):
        scale = row_scale(temper[head_at(heads, where, h)], head_dim)
        factors[h : h + 1] = scale * scale * (0.5 * LOG2E)
        both[h] = split_directions(directions[h], scale)
    for h in range(heads):
        part, total = head_sums(h, out, both, factors[h : h + 1], own_hidden)
        sums[h * head_dim : (h + 1) * head_dim] = part
        totals.append(total)
    totals.append(jnp.zeros((EXTRA - heads, count), F32))
    sums[heads * head_dim :] = jnp.concatenate(totals, axis=0)
    write_bias(groups, mine, where, src, used, fill, bias)
    for item in on_out:
        item.wait()


def write_bias(groups, mine, where, src, used, fill, bias):
    blocks = groups * mine
    slots = src.shape[1]
    odd = lax.rem(where[0], 2)
    parts = [where[0], where[0] + 1 - 2 * odd, where[0] - 1 + 2 * odd]
    order = [
        lax.rem(where[1] + k, groups) * mine + t for k in range(groups) for t in range(mine)
    ]
    lane = lax.broadcasted_iota(jnp.int32, (1, BLK), 1)
    for i, b in enumerate(order):
        for j, part in enumerate(parts):
            for k, c in enumerate(order):
                block = part * blocks + c
                times = jnp.int32(0)
                for s in range(slots):
                    hit = (s < used[b]) & (src[b, s] == block)
                    times = times + hit.astype(jnp.int32)
                real = jnp.where(times > 0, fill[jnp.clip(block, 0, fill.shape[0] - 1)], 0)
                level = jnp.maximum(jnp.full((1, BLK), times, jnp.int32), 1).astype(F32)
                cols = slice((j * blocks + k) * BLK, (j * blocks + k + 1) * BLK)
                bias[i : i + 1, cols] = jnp.where(lane < real, jnp.log(level) * LOG2E, NEG)


def bundle(chosen, out, both, factors, hidden, sums):
    head_dim = both.shape[1] // 2
    inner = sums.shape[0] - EXTRA
    parts, totals = [], []
    for h in chosen:
        part, total = head_sums(h, out, both, factors[h : h + 1], hidden[...])
        parts.append(part + sums[h * head_dim : (h + 1) * head_dim])
        totals.append(total + sums[inner + h : inner + h + 1])
    spare = jnp.zeros((EXTRA - len(totals), sums.shape[1]), F32)
    return jnp.concatenate(parts + totals + [spare], axis=0)


def rest_kernel(feats, own, gain, w, qkv, pair):
    qkv[...] = dot_nn(norm_rows(feats[...], gain[...]), w[...]).astype(BF16)
    pair[: own.shape[0]] = own[...]
    pair[own.shape[0] :] = feats[...]


def sums_kernel(chosen, qkv, both, factors, hidden, sums, out):
    out[...] = bundle(chosen, qkv, both, factors, hidden, sums).astype(out.dtype)


def near_kernel(near, gain, w, own, rest, kv):
    rows = kv.shape[0] // 2
    mine = own.shape[0]
    kv[:mine] = own[...]
    kv[mine:rows] = rest[...]
    kv[rows:] = dot_nn(norm_rows(near[...], gain[...]), w[...]).astype(BF16)


def phi_kernel(kv, both, factors, phi_q):
    heads, rows = phi_q.shape[:2]
    head_dim = both.shape[1] // 2
    for h in range(heads):
        query = kv[:rows, h * 3 * head_dim : h * 3 * head_dim + head_dim]
        phi_q[h] = features(query, both[h], factors[h : h + 1]).astype(BF16)


def far_kernel(far_own, far_rest, gain, w, kv):
    at = 0
    for part in (far_own, far_rest):
        size = part.shape[0]
        kv[at : at + size] = dot_nn(norm_rows(part[...], gain[...]), w[...]).astype(BF16)
        at += size


def attend_kernel(head_dim, chosen, kv, far, bias, local):
    rows = far.shape[0]
    for i, h in enumerate(chosen):
        at = h * 3 * head_dim
        query = kv[:rows, at : at + head_dim]
        key = kv[:, at + head_dim : at + 2 * head_dim]
        value = kv[:, at + 2 * head_dim : at + 3 * head_dim]
        far_key = far[:, at + head_dim : at + 2 * head_dim]
        far_value = far[:, at + 2 * head_dim : at + 3 * head_dim]
        near_scores, far_scores = dot_nt(query, key), dot_nt(query, far_key)
        parts, totals = [], []
        for b in range(rows // BLK):
            block = slice(b * BLK, (b + 1) * BLK)
            scores = jnp.concatenate([near_scores[block], far_scores[block]], axis=1)
            scores = scores * (head_dim ** (-0.5) * LOG2E) + bias[b : b + 1, :]
            top = jnp.max(scores, axis=1, keepdims=True)
            weights = jnp.exp2(scores - top)
            totals.append(jnp.sum(weights, axis=1, keepdims=True))
            parts.append(weights.astype(BF16))
        weights = jnp.concatenate(parts, axis=0)
        accum = dot_nn(weights[:, : 2 * rows], value) + dot_nn(weights[:, 2 * rows :], far_value)
        local[:, i * head_dim : (i + 1) * head_dim] = accum / jnp.concatenate(totals, axis=0)


def mix_kernel(chosen, phi_q, sums, local, *refs):
    *before, keep, send = refs
    rows = keep.shape[0]
    head_dim = local.shape[1] // len(chosen)
    start = 0
    if before:
        start = before[0].shape[1]
        keep[:, :start] = before[0][...]
        send[:, :, :start] = before[1][...]
    split = sums.shape[1] // 2
    totals = sums[len(chosen) * head_dim :, :].astype(F32)
    for i, h in enumerate(chosen):
        cols = slice(i * head_dim, (i + 1) * head_dim)
        low, high = phi_q[h, :, :split], phi_q[h, :, split:]
        part = sums[cols, :]
        numer = dot_nt(low, part[:, :split]) + dot_nt(high, part[:, split:])
        total = totals[i : i + 1]
        denom = low.astype(F32) * total[:, :split] + high.astype(F32) * total[:, split:]
        denom = jnp.sum(denom, axis=1, keepdims=True)
        mixed = (local[:, cols] + numer / denom).astype(BF16)
        cols = slice(start + i * head_dim, start + (i + 1) * head_dim)
        keep[:, cols] = mixed[:rows]
        for k in range(send.shape[0]):
            send[k, :, cols] = mixed[(k + 1) * rows : (k + 2) * rows]


def early_kernel(keep, w, out):
    out[...] = dot_nn(keep[...], w[: keep.shape[1], :])


def late_kernel(first, *refs):
    parts, w, out = refs[:-2], refs[-2], refs[-1]
    width = parts[0].shape[1]
    total = first[...]
    for k, part in enumerate(parts):
        total = total + dot_nn(part[...], w[(k + 1) * width : (k + 2) * width, :])
    out[...] = total.astype(BF16)


def call(body, outs, specs, args, limit, scratch=()):
    shapes = tuple(jax.ShapeDtypeStruct(shape, dtype) for shape, dtype in outs)
    result = pl.pallas_call(
        body,
        out_shape=shapes,
        in_specs=specs,
        out_specs=(VM,) * len(shapes),
        scratch_shapes=list(scratch),
        compiler_params=pltpu.CompilerParams(vmem_limit_bytes=limit),
        cost_estimate=pl.CostEstimate(flops=0, bytes_accessed=0, transcendentals=0),
    )(*args)
    return result if len(outs) > 1 else result[0]


def shards(
    node_feats, norm_gain, w_qkv, w_out, rand_feat, temper, edge_src, edge_count, block_fill
):
    groups = lax.axis_size("head")
    doms = lax.axis_size("dom")
    heads, head_dim, count = rand_feat.shape
    mine, width = node_feats.shape
    rows = mine * groups
    inner = heads * head_dim
    cols = w_qkv.shape[1]
    limit = (32 if rows <= 256 else 56) * 1024 * 1024
    gain = norm_gain.reshape(1, width)
    where = jnp.stack([lax.axis_index("dom"), lax.axis_index("head")]).astype(jnp.int32)

    def shifted(array, step):
        return lax.ppermute(array, "head", [(i, (i + step) % groups) for i in range(groups)])

    def gathered(array):
        arrived = [shifted(array, groups - k) for k in range(1, groups)]
        return arrived[0] if groups == 2 else jnp.concatenate(arrived, axis=0)

    def crossed(array, bit):
        return lax.ppermute(array, "dom", [(i, i ^ bit) for i in range(doms)])

    def pinned(array):
        return pltpu.with_memory_space_constraint(array, pltpu.HBM)

    rest = gathered(node_feats)
    turns = 2 if heads % 2 == 0 else 1
    if heads == 1:
        temper = jnp.concatenate([temper, temper])
    qkv_own, sums, gain, w_qkv, both, w_out, factors, hidden, bias = call(
        functools.partial(own_kernel, heads, groups),
        [
            ((mine, cols), BF16),
            ((inner + EXTRA, count), F32),
            ((1, width), F32),
            ((width, cols), BF16),
            ((heads, 2 * head_dim, count), BF16),
            (w_out.shape, BF16),
            ((heads, 1), F32),
            ((rows - mine, 1), F32),
            ((rows // BLK, 3 * rows), F32),
        ],
        [SM] + [HB] * 9,
        (
            where, pinned(temper), pinned(block_fill), pinned(edge_src), pinned(edge_count),
            pinned(node_feats), pinned(gain), pinned(w_qkv), pinned(rand_feat), pinned(w_out),
        ),
        limit,
        scratch=[
            pltpu.VMEM(node_feats.shape, BF16),
            pltpu.VMEM(rand_feat.shape, F32),
            pltpu.SMEM(temper.shape, F32),
            pltpu.SMEM(block_fill.shape, jnp.int32),
            pltpu.SMEM(edge_src.shape, jnp.int32),
            pltpu.SMEM(edge_count.shape, jnp.int32),
            pltpu.SemaphoreType.DMA((6 + (2 + groups) * turns,)),
        ],
    )
    pairs = [(i, (i + 1) % doms) for i in range(1, doms, 2)]
    far_own = lax.ppermute(node_feats, "dom", pairs + [(b, a) for a, b in pairs])
    qkv_rest, pair = call(
        rest_kernel,
        [((rows - mine, cols), BF16), ((rows, width), BF16)],
        [VM] * 4,
        (rest, node_feats, gain, w_qkv),
        limit,
    )

    def summed(chosen, dtype):
        return call(
            functools.partial(sums_kernel, chosen),
            [((len(chosen) * head_dim + EXTRA, count), dtype)],
            [VM] * 5,
            (qkv_rest, both, factors, hidden, sums),
            limit,
        )

    def halved(array, chosen):
        at = (array.shape[0] - EXTRA) // 2
        low, high, total = array[:at], array[at : 2 * at], array[2 * at :]
        kept, sent = jnp.where(chosen, high, low), jnp.where(chosen, low, high)
        return [jnp.concatenate([part, total], axis=0) for part in (kept, sent)]

    def joined(mine, other, chosen):
        at = mine.shape[0] - EXTRA
        low, high = jnp.where(chosen, other, mine)[:at], jnp.where(chosen, mine, other)[:at]
        return jnp.concatenate([low, high, mine[at:]], axis=0)

    if turns == 2:
        send = summed(range(heads // 2, heads), BF16)
        keep = summed(range(heads // 2), F32)
    else:
        keep, send = halved(summed(range(heads), F32), where[0] % 2 == 1)
        send = send.astype(BF16)
    got = crossed(send, 1)
    near = crossed(pair, 1)
    got, far_own = lax.optimization_barrier((got, far_own))
    keep = keep + got.astype(F32)
    kv = call(
        near_kernel,
        [((2 * rows, cols), BF16)],
        [VM] * 5,
        (near, gain, w_qkv, qkv_own, qkv_rest),
        limit,
    )
    phi_q = call(
        phi_kernel, [((heads, rows, count), BF16)], [VM] * 3, (kv, both, factors), limit
    )
    sent = keep.astype(BF16)
    first, second, third = [crossed(sent, bit) for bit in (6, 4, 2)]
    first, second, third, kv, phi_q = lax.optimization_barrier((first, second, third, kv, phi_q))
    keep = keep + first.astype(F32) + second.astype(F32) + third.astype(F32)
    far_rest = gathered(far_own)
    far = call(
        far_kernel, [((rows, cols), BF16)], [VM] * 4, (far_own, far_rest, gain, w_qkv), limit
    )
    locals_ = [
        call(
            functools.partial(
                attend_kernel, head_dim, range(t * heads // turns, (t + 1) * heads // turns)
            ),
            [((rows, inner // turns), F32)],
            [VM] * 3,
            (kv, far, bias),
            limit,
        )
        for t in range(turns)
    ]
    bit = 8
    while bit < doms:
        got = crossed(keep.astype(BF16), bit)
        if bit == 8:
            got, *locals_ = lax.optimization_barrier((got, *locals_))
        keep = keep + got.astype(F32)
        bit *= 2
    half = keep.astype(BF16)
    other = crossed(half, 1)
    if turns == 2:
        sums = [half, other]
    else:
        sums = [joined(half, other, where[0] % 2 == 1)]
    done = []
    for t in range(turns):
        chosen = range(t * heads // turns, (t + 1) * heads // turns)
        width_out = chosen[-1] * head_dim + head_dim
        done = call(
            functools.partial(mix_kernel, chosen),
            [((mine, width_out), BF16), ((groups - 1, mine, width_out), BF16)],
            [VM] * (3 + len(done)),
            (phi_q, sums[t], locals_[t], *done),
            limit,
        )
    keep, send = done
    returned = [shifted(send[k - 1], k) for k in range(1, groups)]
    first = call(
        early_kernel, [((mine, w_out.shape[1]), F32)], [VM] * 2, (keep, w_out), limit
    )
    return call(
        late_kernel,
        [((mine, w_out.shape[1]), BF16)],
        [VM] * (1 + groups),
        (first, *returned, w_out),
        limit,
    )


def solution(mesh):
    return jax.shard_map(
        shards,
        mesh=mesh,
        in_specs=(
            P(("dom", "head"), None),
            P(),
            P(None, "head"),
            P(),
            P("head", None, None),
            P("head"),
            P("dom", None),
            P("dom"),
            P(),
        ),
        out_specs=P(("dom", "head"), None),
        check_vma=False,
    )
```

profile of v0, /device:TPU:0, one launch (start us, length us, event | category | flops | bytes accessed | tf_op | source)
XLA Modules:
  0.0 31.5 jit_solution(8374816749418861349)
XLA Ops:
  0.0 3.0 %collective-permute-start = (bf16[128,512]{1,0:T(8,128)(2,1)}, bf16[128,512]{1,0:T(8,128)(2,1)S(1)}, u32[]{:S(2)}, u32[]{:S(2)}) collective-permute-start(bf16[128,512]{1,0:T(8,128)(2,1)} %own.1), channel_id=1, source_target_pairs={{0,1},{1,0},{2,3},{3,2},{4,5},{5,4},{6,7},{7,6},{8,9},{9,8},{10,11... | collective-permute-start | bytes 393224 | tf_op jit(solution)/shard_map/ppermute | solution.py:318
  3.0 3.7 %collective-permute-start.2 = (bf16[128,512]{1,0:T(8,128)(2,1)}, bf16[128,512]{1,0:T(8,128)(2,1)S(1)}, u32[]{:S(2)}, u32[]{:S(2)}) collective-permute-start(bf16[128,512]{1,0:T(8,128)(2,1)} %own.1), channel_id=1, source_target_pairs={{2,4},{6,8},{10,12},{14,16},{18,20},{22,24},{26,28},{30,0},{4,2},{... | collective-permute-start | bytes 393224 | tf_op jit(solution)/shard_map/ppermute | solution.py:364
  6.7 3.2 %shard_map.91 = (bf16[128,768]{1,0:T(8,128)(2,1)S(1)}, f32[264,256]{1,0:T(8,128)S(1)}, f32[1,512]{1,0:T(1,128)S(1)}, bf16[512,768]{1,0:T(8,128)(2,1)S(1)}, bf16[...) custom-call(s32[2]{0:T(128)S(1)} %pad_add_fusion.where, ...), custom_call_target="tpu_custom_call" | custom-call | tf_op jit(solution)/shard_map/pallas_call | solution.py:291
  9.9 0.4 %shard_map.92 = (bf16[128,768]{1,0:T(8,128)(2,1)S(1)}, bf16[256,512]{1,0:T(8,128)(2,1)S(1)}) custom-call(bf16[128,512]{1,0:T(8,128)(2,1)S(1)} %collective-permute-done.feats, bf16[128,512]{1,0:T(8,128)(2,1)S(1)} %copy-done, f32[1,512]{1,0:T(1,128)S(1)} %get-tuple-element.30.gain, bf16[512,768]{1,0:T(8,128)(2,1)S(1)} %get-tuple-element.31.w), custom_call_target="tpu_custom_call" | custom-call | tf_op jit(solution)/shard_map/pallas_call | solution.py:291
  10.4 0.6 %shard_map.94 = bf16[136,256]{1,0:T(8,128)(2,1)S(1)} custom-call(bf16[128,768]{1,0:T(8,128)(2,1)S(1)} %get-tuple-element.32.qkv.rest, bf16[4,128,256]{2,1,0:T(8,128)(2,1)S(1)} %get-tuple-element.33.both, f32[4,1]{1,0:T(4,128)S(1)} %get-tuple-element.34.factors, f32[128,1]{1,0:T(8,128)S(1)} %get-tuple-element.35.hidden, f32[264,256]{1,0:T(8,128)S(1)} %get-tuple-element.36.sums), custom_call_target="tpu_custom_call" | custom-call | tf_op jit(solution)/shard_map/pallas_call | solution.py:291
  11.0 0.6 %shard_map.93 = f32[136,256]{1,0:T(8,128)S(1)} custom-call(bf16[128,768]{1,0:T(8,128)(2,1)S(1)} %get-tuple-element.32.qkv.rest, bf16[4,128,256]{2,1,0:T(8,128)(2,1)S(1)} %get-tuple-element.33.both, f32[4,1]{1,0:T(4,128)S(1)} %get-tuple-element.34.factors, f32[128,1]{1,0:T(8,128)S(1)} %get-tuple-element.35.hidden, f32[264,256]{1,0:T(8,128)S(1)} %get-tuple-element.36.sums), custom_call_target="tpu_custom_call" | custom-call | tf_op jit(solution)/shard_map/pallas_call | solution.py:291
  11.6 0.6 %collective-permute-start.6 = (bf16[256,512]{1,0:T(8,128)(2,1)S(1)}, bf16[256,512]{1,0:T(8,128)(2,1)S(1)}, u32[]{:S(2)}, u32[]{:S(2)}) collective-permute-start(bf16[256,512]{1,0:T(8,128)(2,1)S(1)} %get-tuple-element.38), channel_id=1, source_target_pairs={{0,2},{2,0},{4,6},{6,4},{8,10},{10,8},{12,14},{14,12},{16,18},{18,... | collective-permute-start | bytes 786440 | tf_op jit(solution)/shard_map/ppermute | solution.py:325
  12.5 0.4 %collective-permute-start.4 = (bf16[136,256]{1,0:T(8,128)(2,1)S(1)}, bf16[136,256]{1,0:T(8,128)(2,1)S(1)}, u32[]{:S(2)}, u32[]{:S(2)}) collective-permute-start(bf16[136,256]{1,0:T(8,128)(2,1)S(1)} %fusion), channel_id=1, source_target_pairs={{0,8},{2,10},{4,12},{6,14},{8,0},{10,2},{12,4},{14,6},{16,24},{18,... | collective-permute-start | bytes 208904 | tf_op jit(solution)/shard_map/ppermute | solution.py:325
  12.9 2.9 %collective-permute-start.5 = (bf16[136,256]{1,0:T(8,128)(2,1)S(1)}, bf16[136,256]{1,0:T(8,128)(2,1)S(1)}, u32[]{:S(2)}, u32[]{:S(2)}) collective-permute-start(bf16[136,256]{1,0:T(8,128)(2,1)S(1)} %fusion), channel_id=1, source_target_pairs={{0,4},{2,6},{4,0},{6,2},{8,12},{10,14},{12,8},{14,10},{16,20},{18,... | collective-permute-start | bytes 208904 | tf_op jit(solution)/shard_map/ppermute | solution.py:325
  15.9 0.5 %collective-permute-start.8 = (bf16[128,512]{1,0:T(8,128)(2,1)S(1)}, bf16[128,512]{1,0:T(8,128)(2,1)S(1)}, u32[]{:S(2)}, u32[]{:S(2)}) collective-permute-start(bf16[128,512]{1,0:T(8,128)(2,1)S(1)} %collective-permute-done.2.far_own), channel_id=1, source_target_pairs={{0,1},{1,0},{2,3},{3,2},{4,5},{5,4},{6,7},{7,6},{8,9},{9,8},{10,11... | collective-permute-start | bytes 393224 | tf_op jit(solution)/shard_map/ppermute | solution.py:318
  16.4 0.6 %shard_map.95.kv = bf16[512,768]{1,0:T(8,128)(2,1)S(1)} custom-call(bf16[256,512]{1,0:T(8,128)(2,1)S(1)} %collective-permute-done.6.near, f32[1,512]{1,0:T(1,128)S(1)} %get-tuple-element.30.gain, bf16[512,768]{1,0:T(8,128)(2,1)S(1)} %get-tuple-element.31.w, bf16[128,768]{1,0:T(8,128)(2,1)S(1)} %get-tuple-element.39.own, ...), custom_call_target="tpu_custom_call" | custom-call | tf_op jit(solution)/shard_map/pallas_call | solution.py:291
  17.0 0.6 %shard_map.96.phi_q = bf16[4,256,256]{2,1,0:T(8,128)(2,1)S(1)} custom-call(bf16[512,768]{1,0:T(8,128)(2,1)S(1)} %shard_map.95.kv, bf16[4,128,256]{2,1,0:T(8,128)(2,1)S(1)} %get-tuple-element.33.both, f32[4,1]{1,0:T(4,128)S(1)} %get-tuple-element.34.factors), custom_call_target="tpu_custom_call" | custom-call | tf_op jit(solution)/shard_map/pallas_call | solution.py:291
  17.6 0.6 %collective-permute-done.3 = bf16[136,256]{1,0:T(8,128)(2,1)S(1)} collective-permute-done((bf16[136,256]{1,0:T(8,128)(2,1)S(1)}, bf16[136,256]{1,0:T(8,128)(2,1)S(1)}, u32[]{:S(2)}, u32[]{:S(2)}) %collective-permute-start.3) | collective-permute-done | bytes 69664 | tf_op jit(solution)/shard_map/ppermute | solution.py:325
  18.3 0.7 %collective-permute-done.5 = bf16[136,256]{1,0:T(8,128)(2,1)S(1)} collective-permute-done((bf16[136,256]{1,0:T(8,128)(2,1)S(1)}, bf16[136,256]{1,0:T(8,128)(2,1)S(1)}, u32[]{:S(2)}, u32[]{:S(2)}) %collective-permute-start.5) | collective-permute-done | bytes 69664 | tf_op jit(solution)/shard_map/ppermute | solution.py:325
  19.1 0.9 %collective-permute-start.7 = (bf16[136,256]{1,0:T(8,128)(2,1)S(1)}, bf16[136,256]{1,0:T(8,128)(2,1)S(1)}, u32[]{:S(2)}, u32[]{:S(2)}) collective-permute-start(bf16[136,256]{1,0:T(8,128)(2,1)S(1)} %fusion.1), channel_id=1, source_target_pairs={{0,16},{2,18},{4,20},{6,22},{8,24},{10,26},{12,28},{14,30},{16,0},... | collective-permute-start | bytes 208904 | tf_op jit(solution)/shard_map/ppermute | solution.py:325
  20.0 0.9 %collective-permute-done.8.far_rest = bf16[128,512]{1,0:T(8,128)(2,1)S(1)} collective-permute-done((bf16[128,512]{1,0:T(8,128)(2,1)S(1)}, bf16[128,512]{1,0:T(8,128)(2,1)S(1)}, u32[]{:S(2)}, u32[]{:S(2)}) %collective-permute-start.8) | collective-permute-done | bytes 131104 | tf_op jit(solution)/shard_map/ppermute | solution.py:318
  20.8 0.6 %shard_map.97.far = bf16[256,768]{1,0:T(8,128)(2,1)S(1)} custom-call(bf16[128,512]{1,0:T(8,128)(2,1)S(1)} %collective-permute-done.2.far_own, bf16[128,512]{1,0:T(8,128)(2,1)S(1)} %collective-permute-done.8.far_rest, f32[1,512]{1,0:T(1,128)S(1)} %get-tuple-element.30.gain, bf16[512,768]{1,0:T(8,128)(2,1)S(1)} %get-tuple-element.31.w), custom_call_target="tpu_custom_call" | custom-call | tf_op jit(solution)/shard_map/pallas_call | solution.py:291
  21.4 1.2 %shard_map.98.local = f32[256,128]{1,0:T(8,128)S(1)} custom-call(bf16[512,768]{1,0:T(8,128)(2,1)S(1)} %shard_map.95.kv, bf16[256,768]{1,0:T(8,128)(2,1)S(1)} %shard_map.97.far, f32[2,768]{1,0:T(2,128)S(1)} %get-tuple-element.46.bias), custom_call_target="tpu_custom_call" | custom-call | tf_op jit(solution)/shard_map/pallas_call | solution.py:291
  22.6 1.2 %shard_map.99.local = f32[256,128]{1,0:T(8,128)S(1)} custom-call(bf16[512,768]{1,0:T(8,128)(2,1)S(1)} %shard_map.95.kv, bf16[256,768]{1,0:T(8,128)(2,1)S(1)} %shard_map.97.far, f32[2,768]{1,0:T(2,128)S(1)} %get-tuple-element.46.bias), custom_call_target="tpu_custom_call" | custom-call | tf_op jit(solution)/shard_map/pallas_call | solution.py:291
  23.8 0.8 %collective-permute-done.7 = bf16[136,256]{1,0:T(8,128)(2,1)S(1)} collective-permute-done((bf16[136,256]{1,0:T(8,128)(2,1)S(1)}, bf16[136,256]{1,0:T(8,128)(2,1)S(1)}, u32[]{:S(2)}, u32[]{:S(2)}) %collective-permute-start.7) | collective-permute-done | bytes 69664 | tf_op jit(solution)/shard_map/ppermute | solution.py:325
  25.1 0.9 %collective-permute-done.9.sums = bf16[136,256]{1,0:T(8,128)(2,1)S(1)} collective-permute-done((bf16[136,256]{1,0:T(8,128)(2,1)S(1)}, bf16[136,256]{1,0:T(8,128)(2,1)S(1)}, u32[]{:S(2)}, u32[]{:S(2)}) %collective-permute-start.9) | collective-permute-done | bytes 69664 | tf_op jit(solution)/shard_map/ppermute | solution.py:325
  26.3 0.6 %collective-permute-start.10 = (bf16[128,256]{1,0:T(8,128)(2,1)S(1)}, bf16[128,256]{1,0:T(8,128)(2,1)S(1)}, u32[]{:S(2)}, u32[]{:S(2)}) collective-permute-start(bf16[128,256]{1,0:T(8,128)(2,1)S(1)} %bitcast.4), channel_id=1, source_target_pairs={{0,1},{1,0},{2,3},{3,2},{4,5},{5,4},{6,7},{7,6},{8,9},{9,8},{10,11... | collective-permute-start | bytes 196616 | tf_op jit(solution)/shard_map/ppermute | solution.py:318
  27.1 3.5 %collective-permute-done.10.refs_0_ = bf16[128,256]{1,0:T(8,128)(2,1)S(1)} collective-permute-done((bf16[128,256]{1,0:T(8,128)(2,1)S(1)}, bf16[128,256]{1,0:T(8,128)(2,1)S(1)}, u32[]{:S(2)}, u32[]{:S(2)}) %collective-permute-start.10) | collective-permute-done | bytes 65568 | tf_op jit(solution)/shard_map/ppermute | solution.py:318
  30.6 0.8 %shard_map.103 = bf16[128,512]{1,0:T(8,128)(2,1)} custom-call(f32[128,512]{1,0:T(8,128)S(1)} %shard_map.102.first, bf16[128,256]{1,0:T(8,128)(2,1)S(1)} %collective-permute-done.10.refs_0_, bf16[512,512]{1,0:T(8,128)(2,1)S(1)} %get-tuple-element.53.w.refs_1_), custom_call_target="tpu_custom_call" | custom-call | tf_op jit(solution)/shard_map/pallas_call | solution.py:291
  (17 shorter events, 1.4 us)
Async XLA Ops:
  0.0 9.9 %collective-permute-start = (bf16[128,512]{1,0:T(8,128)(2,1)}, bf16[128,512]{1,0:T(8,128)(2,1)S(1)}, u32[]{:S(2)}, u32[]{:S(2)}) collective-permute-start(bf16[128,512]{1,0:T(8,128)(2,1)} %own.1), channel_id=1, source_target_pairs={{0,1},{1,0},{2,3},{3,2},{4,5},{5,4},{6,7},{7,6},{8,9},{9,8},{10,11... | collective-permute-start | bytes 393224 | tf_op jit(solution)/shard_map/ppermute | solution.py:318
  3.0 9.2 %collective-permute-start.2 = (bf16[128,512]{1,0:T(8,128)(2,1)}, bf16[128,512]{1,0:T(8,128)(2,1)S(1)}, u32[]{:S(2)}, u32[]{:S(2)}) collective-permute-start(bf16[128,512]{1,0:T(8,128)(2,1)} %own.1), channel_id=1, source_target_pairs={{2,4},{6,8},{10,12},{14,16},{18,20},{22,24},{26,28},{30,0},{4,2},{... | collective-permute-start | bytes 393224 | tf_op jit(solution)/shard_map/ppermute | solution.py:364
  6.7 3.2 %copy-start = (bf16[128,512]{1,0:T(8,128)(2,1)S(1)}, bf16[128,512]{1,0:T(8,128)(2,1)}, u32[]{:S(2)}) copy-start(bf16[128,512]{1,0:T(8,128)(2,1)} %own.1) | copy-start | bytes 393220
  11.0 1.3 %collective-permute-start.1 = (bf16[136,256]{1,0:T(8,128)(2,1)S(1)}, bf16[136,256]{1,0:T(8,128)(2,1)S(1)}, u32[]{:S(2)}, u32[]{:S(2)}) collective-permute-start(bf16[136,256]{1,0:T(8,128)(2,1)S(1)} %shard_map.94), channel_id=1, source_target_pairs={{0,2},{2,0},{4,6},{6,4},{8,10},{10,8},{12,14},{14,12},{16,18},{18,... | collective-permute-start | bytes 208904 | tf_op jit(solution)/shard_map/ppermute | solution.py:325
  11.6 4.8 %collective-permute-start.6 = (bf16[256,512]{1,0:T(8,128)(2,1)S(1)}, bf16[256,512]{1,0:T(8,128)(2,1)S(1)}, u32[]{:S(2)}, u32[]{:S(2)}) collective-permute-start(bf16[256,512]{1,0:T(8,128)(2,1)S(1)} %get-tuple-element.38), channel_id=1, source_target_pairs={{0,2},{2,0},{4,6},{6,4},{8,10},{10,8},{12,14},{14,12},{16,18},{18,... | collective-permute-start | bytes 786440 | tf_op jit(solution)/shard_map/ppermute | solution.py:325
  12.3 6.0 %collective-permute-start.3 = (bf16[136,256]{1,0:T(8,128)(2,1)S(1)}, bf16[136,256]{1,0:T(8,128)(2,1)S(1)}, u32[]{:S(2)}, u32[]{:S(2)}) collective-permute-start(bf16[136,256]{1,0:T(8,128)(2,1)S(1)} %fusion), channel_id=1, source_target_pairs={{0,12},{2,14},{4,8},{6,10},{8,4},{10,6},{12,0},{14,2},{16,28},{18,... | collective-permute-start | bytes 208904 | tf_op jit(solution)/shard_map/ppermute | solution.py:325
  12.5 5.8 %collective-permute-start.4 = (bf16[136,256]{1,0:T(8,128)(2,1)S(1)}, bf16[136,256]{1,0:T(8,128)(2,1)S(1)}, u32[]{:S(2)}, u32[]{:S(2)}) collective-permute-start(bf16[136,256]{1,0:T(8,128)(2,1)S(1)} %fusion), channel_id=1, source_target_pairs={{0,8},{2,10},{4,12},{6,14},{8,0},{10,2},{12,4},{14,6},{16,24},{18,... | collective-permute-start | bytes 208904 | tf_op jit(solution)/shard_map/ppermute | solution.py:325
  12.9 6.1 %collective-permute-start.5 = (bf16[136,256]{1,0:T(8,128)(2,1)S(1)}, bf16[136,256]{1,0:T(8,128)(2,1)S(1)}, u32[]{:S(2)}, u32[]{:S(2)}) collective-permute-start(bf16[136,256]{1,0:T(8,128)(2,1)S(1)} %fusion), channel_id=1, source_target_pairs={{0,4},{2,6},{4,0},{6,2},{8,12},{10,14},{12,8},{14,10},{16,20},{18,... | collective-permute-start | bytes 208904 | tf_op jit(solution)/shard_map/ppermute | solution.py:325
  15.9 5.0 %collective-permute-start.8 = (bf16[128,512]{1,0:T(8,128)(2,1)S(1)}, bf16[128,512]{1,0:T(8,128)(2,1)S(1)}, u32[]{:S(2)}, u32[]{:S(2)}) collective-permute-start(bf16[128,512]{1,0:T(8,128)(2,1)S(1)} %collective-permute-done.2.far_own), channel_id=1, source_target_pairs={{0,1},{1,0},{2,3},{3,2},{4,5},{5,4},{6,7},{7,6},{8,9},{9,8},{10,11... | collective-permute-start | bytes 393224 | tf_op jit(solution)/shard_map/ppermute | solution.py:318
  19.1 5.6 %collective-permute-start.7 = (bf16[136,256]{1,0:T(8,128)(2,1)S(1)}, bf16[136,256]{1,0:T(8,128)(2,1)S(1)}, u32[]{:S(2)}, u32[]{:S(2)}) collective-permute-start(bf16[136,256]{1,0:T(8,128)(2,1)S(1)} %fusion.1), channel_id=1, source_target_pairs={{0,16},{2,18},{4,20},{6,22},{8,24},{10,26},{12,28},{14,30},{16,0},... | collective-permute-start | bytes 208904 | tf_op jit(solution)/shard_map/ppermute | solution.py:325
  24.7 1.3 %collective-permute-start.9 = (bf16[136,256]{1,0:T(8,128)(2,1)S(1)}, bf16[136,256]{1,0:T(8,128)(2,1)S(1)}, u32[]{:S(2)}, u32[]{:S(2)}) collective-permute-start(bf16[136,256]{1,0:T(8,128)(2,1)S(1)} %add_convert_fusion.sums), channel_id=1, source_target_pairs={{0,2},{2,0},{4,6},{6,4},{8,10},{10,8},{12,14},{14,12},{16,18},{18,... | collective-permute-start | bytes 208904 | tf_op jit(solution)/shard_map/ppermute | solution.py:325
  26.3 4.3 %collective-permute-start.10 = (bf16[128,256]{1,0:T(8,128)(2,1)S(1)}, bf16[128,256]{1,0:T(8,128)(2,1)S(1)}, u32[]{:S(2)}, u32[]{:S(2)}) collective-permute-start(bf16[128,256]{1,0:T(8,128)(2,1)S(1)} %bitcast.4), channel_id=1, source_target_pairs={{0,1},{1,0},{2,3},{3,2},{4,5},{5,4},{6,7},{7,6},{8,9},{9,8},{10,11... | collective-permute-start | bytes 196616 | tf_op jit(solution)/shard_map/ppermute | solution.py:318
where the time goes:
time: 31.6 us; the launch traced here: 31.5 us
  starting transfers between devices  12.9 us (41%)
  Pallas kernels  10.6 us (34%)
  waiting for transfers between devices  7.62 us (24%)
    pallas_call x13, Pallas kernels, call(): pl.pallas_call(body, out_shape=shapes, in_specs=specs, out_specs=(VM,) *...  10.6 us
    ppermute x7, starting transfers between devices, crossed(): return lax.ppermute(array, 'dom', [(i, i ^ bit) for i in range(doms)])  5.16 us
    ppermute x3, waiting for transfers between devices, shifted(): lax.ppermute(array, 'head', [(i, (i + step) % groups) for i in range(grou...  4.39 us
    ppermute x3, starting transfers between devices, shifted(): lax.ppermute(array, 'head', [(i, (i + step) % groups) for i in range(grou...  4.1 us
    ppermute x1, starting transfers between devices, shards(): lax.ppermute(node_feats, 'dom', pairs + [(b, a) for a, b in pairs])  3.69 us
    ppermute x7, waiting for transfers between devices, crossed(): return lax.ppermute(array, 'dom', [(i, i ^ bit) for i in range(doms)])  3.24 us
  transfers between devices with their start and end apart: 11, of which 7 were waited for; matrix products, arithmetic and copies ran while one was open for 0% of the time, Pallas kernels for 30%

commit v1 on v0

--- a/solution.py
+++ b/solution.py
@@ -410,10 +410,14 @@
     phi_q = call(
         phi_kernel, [((heads, rows, count), BF16)], [VM] * 3, (kv, both, factors), limit
     )
-    sent = keep.astype(BF16)
-    first, second, third = [crossed(sent, bit) for bit in (6, 4, 2)]
-    first, second, third, kv, phi_q = lax.optimization_barrier((first, second, third, kv, phi_q))
-    keep = keep + first.astype(F32) + second.astype(F32) + third.astype(F32)
+    size = inner // 2 + EXTRA
+    fours = [[i, i + 2, i + 4, i + 6] for i in range(doms) if i % 8 < 2]
+    copies = jnp.broadcast_to(keep.astype(BF16)[None], (4, size, count))
+    got = lax.all_to_all(
+        copies, "dom", split_axis=0, concat_axis=0, axis_index_groups=fours, tiled=True
+    )
+    got, kv, phi_q = lax.optimization_barrier((got, kv, phi_q))
+    keep = jnp.sum(got.astype(F32), axis=0)
     far_rest = gathered(far_own)
     far = call(
         far_kernel, [((rows, cols), BF16)], [VM] * 4, (far_own, far_rest, gain, w_qkv), limit

time: 31.6 us -> 38 us (1.20)
  waiting for transfers between devices: 7.62 us -> 12.7 us
  other arithmetic: 0.2 us -> 1.12 us
  local copies, waits for them, and re-layouts: 0.01 us -> 0.74 us
  starting transfers between devices: 12.9 us -> 12.5 us
    ppermute x7 -> x4, starting transfers between devices: 5.16 us -> 0.63 us  [crossed(): return lax.ppermute(array, 'dom', [(i, i ^ bit) for i in range(doms)])]
    all_to_all x0 -> x1, starting transfers between devices: none -> 4.09 us  [shards(): lax.all_to_all(copies, 'dom', split_axis=0, concat_axis=0, axis_index_gro...]
    all_to_all x0 -> x1, waiting for transfers between devices: none -> 3.3 us  [shards(): lax.all_to_all(copies, 'dom', split_axis=0, concat_axis=0, axis_index_gro...]
    ppermute x7 -> x4, waiting for transfers between devices: 3.24 us -> 5.81 us  [crossed(): return lax.ppermute(array, 'dom', [(i, i ^ bit) for i in range(doms)])]
    reduce_sum x0 -> x1, other arithmetic: none -> 1.01 us  [shards(): keep = jnp.sum(got.astype(F32), axis=0)]
    ppermute x3, waiting for transfers between devices: 4.39 us -> 3.57 us  [shifted(): lax.ppermute(array, 'head', [(i, (i + step) % groups) for i in range(grou...]
    broadcast_in_dim x0 -> x1, local copies, waits for them, and re-layouts: none -> 0.74 us  [shards(): copies = jnp.broadcast_to(keep.astype(BF16)[None], (4, size, count))]
  transfers between devices with their start and end apart: 11 -> 9, of which waited for: 7 -> 6; matrix products, arithmetic and copies ran while one was open for 0% -> 3% of each run, Pallas kernels for 30% -> 25%
where the time goes in v1:
time: 38 us; the launch traced here: 37.7 us
  waiting for transfers between devices  12.7 us (33%)
  starting transfers between devices  12.5 us (33%)
  Pallas kernels  10.5 us (28%)
  other arithmetic  1.12 us (3%)
  local copies, waits for them, and re-layouts  0.74 us (2%)
    pallas_call x13, Pallas kernels, call(): pl.pallas_call(body, out_shape=shapes, in_specs=specs, out_specs=(VM,) *...  10.5 us
    ppermute x4, waiting for transfers between devices, crossed(): return lax.ppermute(array, 'dom', [(i, i ^ bit) for i in range(doms)])  5.81 us
    all_to_all x1, starting transfers between devices, shards(): lax.all_to_all(copies, 'dom', split_axis=0, concat_axis=0, axis_index_gro...  4.09 us
    ppermute x3, starting transfers between devices, shifted(): lax.ppermute(array, 'head', [(i, (i + step) % groups) for i in range(grou...  4.05 us
    ppermute x1, starting transfers between devices, shards(): lax.ppermute(node_feats, 'dom', pairs + [(b, a) for a, b in pairs])  3.69 us
    ppermute x3, waiting for transfers between devices, shifted(): lax.ppermute(array, 'head', [(i, (i + step) % groups) for i in range(grou...  3.57 us
    all_to_all x1, waiting for transfers between devices, shards(): lax.all_to_all(copies, 'dom', split_axis=0, concat_axis=0, axis_index_gro...  3.3 us
    reduce_sum x1, other arithmetic, shards(): keep = jnp.sum(got.astype(F32), axis=0)  1.01 us
  transfers between devices with their start and end apart: 9, of which 6 were waited for; matrix products, arithmetic and copies ran while one was open for 3% of the time, Pallas kernels for 25%

profile of v1, /device:TPU:0, one launch (start us, length us, event | category | flops | bytes accessed | tf_op | source)
XLA Modules:
  0.0 37.7 jit_solution(11059540522700871186)
XLA Ops:
  0.0 3.0 %collective-permute-start = (bf16[128,512]{1,0:T(8,128)(2,1)}, bf16[128,512]{1,0:T(8,128)(2,1)S(1)}, u32[]{:S(2)}, u32[]{:S(2)}) collective-permute-start(bf16[128,512]{1,0:T(8,128)(2,1)} %own.1), channel_id=1, source_target_pairs={{0,1},{1,0},{2,3},{3,2},{4,5},{5,4},{6,7},{7,6},{8,9},{9,8},{10,11... | collective-permute-start | bytes 393224 | tf_op jit(solution)/shard_map/ppermute | solution.py:318
  3.0 3.7 %collective-permute-start.2 = (bf16[128,512]{1,0:T(8,128)(2,1)}, bf16[128,512]{1,0:T(8,128)(2,1)S(1)}, u32[]{:S(2)}, u32[]{:S(2)}) collective-permute-start(bf16[128,512]{1,0:T(8,128)(2,1)} %own.1), channel_id=1, source_target_pairs={{2,4},{6,8},{10,12},{14,16},{18,20},{22,24},{26,28},{30,0},{4,2},{... | collective-permute-start | bytes 393224 | tf_op jit(solution)/shard_map/ppermute | solution.py:364
  6.7 3.2 %shard_map.91 = (bf16[128,768]{1,0:T(8,128)(2,1)S(1)}, f32[264,256]{1,0:T(8,128)S(1)}, f32[1,512]{1,0:T(1,128)S(1)}, bf16[512,768]{1,0:T(8,128)(2,1)S(1)}, bf16[...) custom-call(s32[2]{0:T(128)S(1)} %pad_add_fusion.where, ...), custom_call_target="tpu_custom_call" | custom-call | tf_op jit(solution)/shard_map/pallas_call | solution.py:291
  9.9 0.4 %shard_map.92 = (bf16[128,768]{1,0:T(8,128)(2,1)S(1)}, bf16[256,512]{1,0:T(8,128)(2,1)S(1)}) custom-call(bf16[128,512]{1,0:T(8,128)(2,1)S(1)} %collective-permute-done.feats, bf16[128,512]{1,0:T(8,128)(2,1)S(1)} %copy-done, f32[1,512]{1,0:T(1,128)S(1)} %get-tuple-element.28.gain, bf16[512,768]{1,0:T(8,128)(2,1)S(1)} %get-tuple-element.29.w), custom_call_target="tpu_custom_call" | custom-call | tf_op jit(solution)/shard_map/pallas_call | solution.py:291
  10.4 0.6 %shard_map.94 = bf16[136,256]{1,0:T(8,128)(2,1)S(1)} custom-call(bf16[128,768]{1,0:T(8,128)(2,1)S(1)} %get-tuple-element.30.qkv.rest, bf16[4,128,256]{2,1,0:T(8,128)(2,1)S(1)} %get-tuple-element.31.both, f32[4,1]{1,0:T(4,128)S(1)} %get-tuple-element.32.factors, f32[128,1]{1,0:T(8,128)S(1)} %get-tuple-element.33.hidden, f32[264,256]{1,0:T(8,128)S(1)} %get-tuple-element.34.sums), custom_call_target="tpu_custom_call" | custom-call | tf_op jit(solution)/shard_map/pallas_call | solution.py:291
  11.0 0.6 %shard_map.93 = f32[136,256]{1,0:T(8,128)S(1)} custom-call(bf16[128,768]{1,0:T(8,128)(2,1)S(1)} %get-tuple-element.30.qkv.rest, bf16[4,128,256]{2,1,0:T(8,128)(2,1)S(1)} %get-tuple-element.31.both, f32[4,1]{1,0:T(4,128)S(1)} %get-tuple-element.32.factors, f32[128,1]{1,0:T(8,128)S(1)} %get-tuple-element.33.hidden, f32[264,256]{1,0:T(8,128)S(1)} %get-tuple-element.34.sums), custom_call_target="tpu_custom_call" | custom-call | tf_op jit(solution)/shard_map/pallas_call | solution.py:291
  11.6 0.7 %collective-permute-done.1 = bf16[136,256]{1,0:T(8,128)(2,1)S(1)} collective-permute-done((bf16[136,256]{1,0:T(8,128)(2,1)S(1)}, bf16[136,256]{1,0:T(8,128)(2,1)S(1)}, u32[]{:S(2)}, u32[]{:S(2)}) %collective-permute-start.1) | collective-permute-done | bytes 69664 | tf_op jit(solution)/shard_map/ppermute | solution.py:325
  12.3 0.7 %broadcast_in_dim.2 = bf16[4,136,256]{2,1,0:T(8,128)(2,1)} broadcast(bf16[136,256]{1,0:T(8,128)(2,1)S(1)} %add_convert_fusion.1), dimensions={1,2} | broadcast | bytes 348160 | tf_op jit(solution)/shard_map/broadcast_in_dim | solution.py:415
  13.0 4.1 %all-to-all-start = ((bf16[4,136,256]{2,1,0:T(8,128)(2,1)}), bf16[4,136,256]{2,1,0:T(8,128)(2,1)}, u32[]{:S(2)}, u32[]{:S(2)}) async-start(bf16[4,136,256]{2,1,0:T(8,128)(2,1)} %broadcast_in_dim.2), calls=%async_computation | async-start | bytes 557056 | tf_op jit(solution)/shard_map/all_to_all | solution.py:416
  17.4 0.5 %collective-permute-start.5 = (bf16[128,512]{1,0:T(8,128)(2,1)S(1)}, bf16[128,512]{1,0:T(8,128)(2,1)S(1)}, u32[]{:S(2)}, u32[]{:S(2)}) collective-permute-start(bf16[128,512]{1,0:T(8,128)(2,1)S(1)} %collective-permute-done.2.far_own), channel_id=1, source_target_pairs={{0,1},{1,0},{2,3},{3,2},{4,5},{5,4},{6,7},{7,6},{8,9},{9,8},{10,11... | collective-permute-start | bytes 393224 | tf_op jit(solution)/shard_map/ppermute | solution.py:318
  17.9 0.9 %collective-permute-done.3.near = bf16[256,512]{1,0:T(8,128)(2,1)S(1)} collective-permute-done((bf16[256,512]{1,0:T(8,128)(2,1)S(1)}, bf16[256,512]{1,0:T(8,128)(2,1)S(1)}, u32[]{:S(2)}, u32[]{:S(2)}) %collective-permute-start.3) | collective-permute-done | bytes 262176 | tf_op jit(solution)/shard_map/ppermute | solution.py:325
  18.7 0.6 %shard_map.95.kv = bf16[512,768]{1,0:T(8,128)(2,1)S(1)} custom-call(bf16[256,512]{1,0:T(8,128)(2,1)S(1)} %collective-permute-done.3.near, f32[1,512]{1,0:T(1,128)S(1)} %get-tuple-element.28.gain, bf16[512,768]{1,0:T(8,128)(2,1)S(1)} %get-tuple-element.29.w, bf16[128,768]{1,0:T(8,128)(2,1)S(1)} %get-tuple-element.37.own, ...), custom_call_target="tpu_custom_call" | custom-call | tf_op jit(solution)/shard_map/pallas_call | solution.py:291
  19.3 0.6 %shard_map.96.phi_q = bf16[4,256,256]{2,1,0:T(8,128)(2,1)S(1)} custom-call(bf16[512,768]{1,0:T(8,128)(2,1)S(1)} %shard_map.95.kv, bf16[4,128,256]{2,1,0:T(8,128)(2,1)S(1)} %get-tuple-element.31.both, f32[4,1]{1,0:T(4,128)S(1)} %get-tuple-element.32.factors), custom_call_target="tpu_custom_call" | custom-call | tf_op jit(solution)/shard_map/pallas_call | solution.py:291
  20.0 3.3 %all-to-all-done = bf16[4,136,256]{2,1,0:T(8,128)(2,1)} async-done(((bf16[4,136,256]{2,1,0:T(8,128)(2,1)}), bf16[4,136,256]{2,1,0:T(8,128)(2,1)}, u32[]{:S(2)}, u32[]{:S(2)}) %all-to-all-start) | async-done | bytes 278560 | tf_op jit(solution)/shard_map/all_to_all | solution.py:416
  23.3 1.0 %convert_reduce_fusion = f32[136,256]{1,0:T(8,128)S(1)} fusion(bf16[4,136,256]{2,1,0:T(8,128)(2,1)} %all-to-all-done), kind=kLoop, calls=%fused_computation | loop fusion | flops 243712 | bytes 417792 | tf_op jit(solution)/shard_map/reduce_sum | solution.py:420
  24.6 0.6 %shard_map.97.far = bf16[256,768]{1,0:T(8,128)(2,1)S(1)} custom-call(bf16[128,512]{1,0:T(8,128)(2,1)S(1)} %collective-permute-done.2.far_own, bf16[128,512]{1,0:T(8,128)(2,1)S(1)} %collective-permute-done.5.far_rest, f32[1,512]{1,0:T(1,128)S(1)} %get-tuple-element.28.gain, bf16[512,768]{1,0:T(8,128)(2,1)S(1)} %get-tuple-element.29.w), custom_call_target="tpu_custom_call" | custom-call | tf_op jit(solution)/shard_map/pallas_call | solution.py:291
  25.2 1.2 %shard_map.98.local = f32[256,128]{1,0:T(8,128)S(1)} custom-call(bf16[512,768]{1,0:T(8,128)(2,1)S(1)} %shard_map.95.kv, bf16[256,768]{1,0:T(8,128)(2,1)S(1)} %shard_map.97.far, f32[2,768]{1,0:T(2,128)S(1)} %get-tuple-element.42.bias), custom_call_target="tpu_custom_call" | custom-call | tf_op jit(solution)/shard_map/pallas_call | solution.py:291
  26.4 1.2 %shard_map.99.local = f32[256,128]{1,0:T(8,128)S(1)} custom-call(bf16[512,768]{1,0:T(8,128)(2,1)S(1)} %shard_map.95.kv, bf16[256,768]{1,0:T(8,128)(2,1)S(1)} %shard_map.97.far, f32[2,768]{1,0:T(2,128)S(1)} %get-tuple-element.42.bias), custom_call_target="tpu_custom_call" | custom-call | tf_op jit(solution)/shard_map/pallas_call | solution.py:291
  27.6 3.3 %collective-permute-done.4 = bf16[136,256]{1,0:T(8,128)(2,1)S(1)} collective-permute-done((bf16[136,256]{1,0:T(8,128)(2,1)S(1)}, bf16[136,256]{1,0:T(8,128)(2,1)S(1)}, u32[]{:S(2)}, u32[]{:S(2)}) %collective-permute-start.4) | collective-permute-done | bytes 69664 | tf_op jit(solution)/shard_map/ppermute | solution.py:325
  31.3 0.9 %collective-permute-done.6.sums = bf16[136,256]{1,0:T(8,128)(2,1)S(1)} collective-permute-done((bf16[136,256]{1,0:T(8,128)(2,1)S(1)}, bf16[136,256]{1,0:T(8,128)(2,1)S(1)}, u32[]{:S(2)}, u32[]{:S(2)}) %collective-permute-start.6) | collective-permute-done | bytes 69664 | tf_op jit(solution)/shard_map/ppermute | solution.py:325
  32.2 0.3 shard_map.101
  32.5 0.6 %collective-permute-start.7 = (bf16[128,256]{1,0:T(8,128)(2,1)S(1)}, bf16[128,256]{1,0:T(8,128)(2,1)S(1)}, u32[]{:S(2)}, u32[]{:S(2)}) collective-permute-start(bf16[128,256]{1,0:T(8,128)(2,1)S(1)} %bitcast.4), channel_id=1, source_target_pairs={{0,1},{1,0},{2,3},{3,2},{4,5},{5,4},{6,7},{7,6},{8,9},{9,8},{10,11... | collective-permute-start | bytes 196616 | tf_op jit(solution)/shard_map/ppermute | solution.py:318
  33.3 3.6 %collective-permute-done.7.refs_0_ = bf16[128,256]{1,0:T(8,128)(2,1)S(1)} collective-permute-done((bf16[128,256]{1,0:T(8,128)(2,1)S(1)}, bf16[128,256]{1,0:T(8,128)(2,1)S(1)}, u32[]{:S(2)}, u32[]{:S(2)}) %collective-permute-start.7) | collective-permute-done | bytes 65568 | tf_op jit(solution)/shard_map/ppermute | solution.py:318
  36.9 0.8 %shard_map.103 = bf16[128,512]{1,0:T(8,128)(2,1)} custom-call(f32[128,512]{1,0:T(8,128)S(1)} %shard_map.102.first, bf16[128,256]{1,0:T(8,128)(2,1)S(1)} %collective-permute-done.7.refs_0_, bf16[512,512]{1,0:T(8,128)(2,1)S(1)} %get-tuple-element.49.w.refs_1_), custom_call_target="tpu_custom_call" | custom-call | tf_op jit(solution)/shard_map/pallas_call | solution.py:291
  (15 shorter events, 1.2 us)
Async XLA Ops:
  0.0 9.9 %collective-permute-start = (bf16[128,512]{1,0:T(8,128)(2,1)}, bf16[128,512]{1,0:T(8,128)(2,1)S(1)}, u32[]{:S(2)}, u32[]{:S(2)}) collective-permute-start(bf16[128,512]{1,0:T(8,128)(2,1)} %own.1), channel_id=1, source_target_pairs={{0,1},{1,0},{2,3},{3,2},{4,5},{5,4},{6,7},{7,6},{8,9},{9,8},{10,11... | collective-permute-start | bytes 393224 | tf_op jit(solution)/shard_map/ppermute | solution.py:318
  3.0 8.6 %collective-permute-start.2 = (bf16[128,512]{1,0:T(8,128)(2,1)}, bf16[128,512]{1,0:T(8,128)(2,1)S(1)}, u32[]{:S(2)}, u32[]{:S(2)}) collective-permute-start(bf16[128,512]{1,0:T(8,128)(2,1)} %own.1), channel_id=1, source_target_pairs={{2,4},{6,8},{10,12},{14,16},{18,20},{22,24},{26,28},{30,0},{4,2},{... | collective-permute-start | bytes 393224 | tf_op jit(solution)/shard_map/ppermute | solution.py:364
  6.7 3.2 %copy-start = (bf16[128,512]{1,0:T(8,128)(2,1)S(1)}, bf16[128,512]{1,0:T(8,128)(2,1)}, u32[]{:S(2)}) copy-start(bf16[128,512]{1,0:T(8,128)(2,1)} %own.1) | copy-start | bytes 393220
  11.0 1.3 %collective-permute-start.1 = (bf16[136,256]{1,0:T(8,128)(2,1)S(1)}, bf16[136,256]{1,0:T(8,128)(2,1)S(1)}, u32[]{:S(2)}, u32[]{:S(2)}) collective-permute-start(bf16[136,256]{1,0:T(8,128)(2,1)S(1)} %shard_map.94), channel_id=1, source_target_pairs={{0,2},{2,0},{4,6},{6,4},{8,10},{10,8},{12,14},{14,12},{16,18},{18,... | collective-permute-start | bytes 208904 | tf_op jit(solution)/shard_map/ppermute | solution.py:325
  13.0 10.3 %all-to-all-start = ((bf16[4,136,256]{2,1,0:T(8,128)(2,1)}), bf16[4,136,256]{2,1,0:T(8,128)(2,1)}, u32[]{:S(2)}, u32[]{:S(2)}) async-start(bf16[4,136,256]{2,1,0:T(8,128)(2,1)} %broadcast_in_dim.2), calls=%async_computation | async-start | bytes 557056 | tf_op jit(solution)/shard_map/all_to_all | solution.py:416
  17.1 1.6 %collective-permute-start.3 = (bf16[256,512]{1,0:T(8,128)(2,1)S(1)}, bf16[256,512]{1,0:T(8,128)(2,1)S(1)}, u32[]{:S(2)}, u32[]{:S(2)}) collective-permute-start(bf16[256,512]{1,0:T(8,128)(2,1)S(1)} %get-tuple-element.36), channel_id=1, source_target_pairs={{0,2},{2,0},{4,6},{6,4},{8,10},{10,8},{12,14},{14,12},{16,18},{18,... | collective-permute-start | bytes 786440 | tf_op jit(solution)/shard_map/ppermute | solution.py:325
  17.4 7.2 %collective-permute-start.5 = (bf16[128,512]{1,0:T(8,128)(2,1)S(1)}, bf16[128,512]{1,0:T(8,128)(2,1)S(1)}, u32[]{:S(2)}, u32[]{:S(2)}) collective-permute-start(bf16[128,512]{1,0:T(8,128)(2,1)S(1)} %collective-permute-done.2.far_own), channel_id=1, source_target_pairs={{0,1},{1,0},{2,3},{3,2},{4,5},{5,4},{6,7},{7,6},{8,9},{9,8},{10,11... | collective-permute-start | bytes 393224 | tf_op jit(solution)/shard_map/ppermute | solution.py:318
  24.3 6.6 %collective-permute-start.4 = (bf16[136,256]{1,0:T(8,128)(2,1)S(1)}, bf16[136,256]{1,0:T(8,128)(2,1)S(1)}, u32[]{:S(2)}, u32[]{:S(2)}) collective-permute-start(bf16[136,256]{1,0:T(8,128)(2,1)S(1)} %convert_element_type.21), channel_id=1, source_target_pairs={{0,16},{2,18},{4,20},{6,22},{8,24},{10,26},{12,28},{14,30},{16,0},... | collective-permute-start | bytes 208904 | tf_op jit(solution)/shard_map/ppermute | solution.py:325
  30.9 1.3 %collective-permute-start.6 = (bf16[136,256]{1,0:T(8,128)(2,1)S(1)}, bf16[136,256]{1,0:T(8,128)(2,1)S(1)}, u32[]{:S(2)}, u32[]{:S(2)}) collective-permute-start(bf16[136,256]{1,0:T(8,128)(2,1)S(1)} %add_convert_fusion.sums), channel_id=1, source_target_pairs={{0,2},{2,0},{4,6},{6,4},{8,10},{10,8},{12,14},{14,12},{16,18},{18,... | collective-permute-start | bytes 208904 | tf_op jit(solution)/shard_map/ppermute | solution.py:325
  32.5 4.3 %collective-permute-start.7 = (bf16[128,256]{1,0:T(8,128)(2,1)S(1)}, bf16[128,256]{1,0:T(8,128)(2,1)S(1)}, u32[]{:S(2)}, u32[]{:S(2)}) collective-permute-start(bf16[128,256]{1,0:T(8,128)(2,1)S(1)} %bitcast.4), channel_id=1, source_target_pairs={{0,1},{1,0},{2,3},{3,2},{4,5},{5,4},{6,7},{7,6},{8,9},{9,8},{10,11... | collective-permute-start | bytes 196616 | tf_op jit(solution)/shard_map/ppermute | solution.py:318

commit v2 on v0

--- a/solution.py
+++ b/solution.py
@@ -63,11 +63,11 @@
 
 
 def head_sums(h, out, both, factor, hidden):
-    head_dim = both.shape[1] // 2
+    head_dim = both.shape[0] // 2
     at = h * 3 * head_dim
     key = out[:, at + head_dim : at + 2 * head_dim]
     value = out[:, at + 2 * head_dim : at + 3 * head_dim]
-    phi = features(key, both[h], factor, hidden)
+    phi = features(key, both, factor, hidden)
     return dot_tn(value, phi.astype(BF16)), jnp.sum(phi, axis=0, keepdims=True)
 
 
@@ -144,7 +144,7 @@
         factors[h : h + 1] = scale * scale * (0.5 * LOG2E)
         both[h] = split_directions(directions[h], scale)
     for h in range(heads):
-        part, total = head_sums(h, out, both, factors[h : h + 1], own_hidden)
+        part, total = head_sums(h, out, both[h], factors[h : h + 1], own_hidden)
         sums[h * head_dim : (h + 1) * head_dim] = part
         totals.append(total)
     totals.append(jnp.zeros((EXTRA - heads, count), F32))
@@ -177,12 +177,12 @@
                 bias[i : i + 1, cols] = jnp.where(lane < real, jnp.log(level) * LOG2E, NEG)
 
 
-def bundle(chosen, out, both, factors, hidden, sums):
+def bundle(chosen, first, out, both, factors, hidden, sums):
     head_dim = both.shape[1] // 2
     inner = sums.shape[0] - EXTRA
     parts, totals = [], []
     for h in chosen:
-        part, total = head_sums(h, out, both, factors[h : h + 1], hidden[...])
+        part, total = head_sums(h - first, out, both[h], factors[h : h + 1], hidden[...])
         parts.append(part + sums[h * head_dim : (h + 1) * head_dim])
         totals.append(total + sums[inner + h : inner + h + 1])
     spare = jnp.zeros((EXTRA - len(totals), sums.shape[1]), F32)
@@ -195,8 +195,22 @@
     pair[own.shape[0] :] = feats[...]
 
 
-def sums_kernel(chosen, qkv, both, factors, hidden, sums, out):
-    out[...] = bundle(chosen, qkv, both, factors, hidden, sums).astype(out.dtype)
+def sent_kernel(feats, gain, w, normed, qkv):
+    rows = norm_rows(feats[...], gain[...])
+    normed[...] = rows
+    qkv[...] = dot_nn(rows, w[:, qkv.shape[1] :]).astype(BF16)
+
+
+def kept_kernel(feats, own, normed, upper, w, qkv, pair):
+    half = upper.shape[1]
+    qkv[:, :half] = dot_nn(normed[...], w[:, :half]).astype(BF16)
+    qkv[:, half:] = upper[...]
+    pair[: own.shape[0]] = own[...]
+    pair[own.shape[0] :] = feats[...]
+
+
+def sums_kernel(chosen, first, qkv, both, factors, hidden, sums, out):
+    out[...] = bundle(chosen, first, qkv, both, factors, hidden, sums).astype(out.dtype)
 
 
 def near_kernel(near, gain, w, own, rest, kv):
@@ -257,7 +271,7 @@
         keep[:, :start] = before[0][...]
         send[:, :, :start] = before[1][...]
     split = sums.shape[1] // 2
-    totals = sums[len(chosen) * head_dim :, :].astype(F32)
+    totals = sums[...].astype(F32)[len(chosen) * head_dim :]
     for i, h in enumerate(chosen):
         cols = slice(i * head_dim, (i + 1) * head_dim)
         low, high = phi_q[h, :, :split], phi_q[h, :, split:]
@@ -362,20 +376,14 @@
     )
     pairs = [(i, (i + 1) % doms) for i in range(1, doms, 2)]
     far_own = lax.ppermute(node_feats, "dom", pairs + [(b, a) for a, b in pairs])
-    qkv_rest, pair = call(
-        rest_kernel,
-        [((rows - mine, cols), BF16), ((rows, width), BF16)],
-        [VM] * 4,
-        (rest, node_feats, gain, w_qkv),
-        limit,
-    )
-
-    def summed(chosen, dtype):
+    rest_out = [((rows - mine, cols), BF16), ((rows, width), BF16)]
+
+    def summed(chosen, first, qkv, dtype):
         return call(
-            functools.partial(sums_kernel, chosen),
+            functools.partial(sums_kernel, chosen, first),
             [((len(chosen) * head_dim + EXTRA, count), dtype)],
             [VM] * 5,
-            (qkv_rest, both, factors, hidden, sums),
+            (qkv, both, factors, hidden, sums),
             limit,
         )
 
@@ -391,10 +399,23 @@
         return jnp.concatenate([low, high, mine[at:]], axis=0)
 
     if turns == 2:
-        send = summed(range(heads // 2, heads), BF16)
-        keep = summed(range(heads // 2), F32)
+        normed, upper = call(
+            sent_kernel,
+            [((rows - mine, width), BF16), ((rows - mine, cols // 2), BF16)],
+            [VM] * 3,
+            (rest, gain, w_qkv),
+            limit,
+        )
+        send = summed(range(heads // 2, heads), heads // 2, upper, BF16)
+        qkv_rest, pair = call(
+            kept_kernel, rest_out, [VM] * 5, (rest, node_feats, normed, upper, w_qkv), limit
+        )
+        keep = summed(range(heads // 2), 0, qkv_rest, F32)
     else:
-        keep, send = halved(summed(range(heads), F32), where[0] % 2 == 1)
+        qkv_rest, pair = call(
+            rest_kernel, rest_out, [VM] * 4, (rest, node_feats, gain, w_qkv), limit
+        )
+        keep, send = halved(summed(range(heads), 0, qkv_rest, F32), where[0] % 2 == 1)
         send = send.astype(BF16)
     got = crossed(send, 1)
     near = crossed(pair, 1)
@@ -411,7 +432,7 @@
         phi_kernel, [((heads, rows, count), BF16)], [VM] * 3, (kv, both, factors), limit
     )
     sent = keep.astype(BF16)
-    first, second, third = [crossed(sent, bit) for bit in (6, 4, 2)]
+    first, second, third = [crossed(sent, bit) for bit in (6, 2, 4)]
     first, second, third, kv, phi_q = lax.optimization_barrier((first, second, third, kv, phi_q))
     keep = keep + first.astype(F32) + second.astype(F32) + third.astype(F32)
     far_rest = gathered(far_own)

time: 31.6 us -> 30.9 us (0.978)
  waiting for transfers between devices: 7.62 us -> 5.84 us
  starting transfers between devices: 12.9 us -> 13.6 us
    ppermute x7, waiting for transfers between devices: 3.24 us -> 1.69 us  [crossed(): return lax.ppermute(array, 'dom', [(i, i ^ bit) for i in range(doms)])]
    ppermute x7, starting transfers between devices: 5.16 us -> 5.69 us  [crossed(): return lax.ppermute(array, 'dom', [(i, i ^ bit) for i in range(doms)])]
    pallas_call x13 -> x14, Pallas kernels: 10.6 us -> 10.8 us  [call(): pl.pallas_call(body, out_shape=shapes, in_specs=specs, out_specs=(VM,) *...]
  transfers between devices with their start and end apart: 11 -> 11, of which waited for: 7 -> 5; matrix products, arithmetic and copies ran while one was open for 0% -> 0% of each run, Pallas kernels for 30% -> 31%
where the time goes in v2:
time: 30.9 us; the launch traced here: 30.8 us
  starting transfers between devices  13.6 us (44%)
  Pallas kernels  10.8 us (35%)
  waiting for transfers between devices  5.84 us (19%)
    pallas_call x14, Pallas kernels, call(): pl.pallas_call(body, out_shape=shapes, in_specs=specs, out_specs=(VM,) *...  10.8 us
    ppermute x7, starting transfers between devices, crossed(): return lax.ppermute(array, 'dom', [(i, i ^ bit) for i in range(doms)])  5.69 us
    ppermute x3, starting transfers between devices, shifted(): lax.ppermute(array, 'head', [(i, (i + step) % groups) for i in range(grou...  4.2 us
    ppermute x3, waiting for transfers between devices, shifted(): lax.ppermute(array, 'head', [(i, (i + step) % groups) for i in range(grou...  4.15 us
    ppermute x1, starting transfers between devices, shards(): lax.ppermute(node_feats, 'dom', pairs + [(b, a) for a, b in pairs])  3.69 us
    ppermute x7, waiting for transfers between devices, crossed(): return lax.ppermute(array, 'dom', [(i, i ^ bit) for i in range(doms)])  1.69 us
  transfers between devices with their start and end apart: 11, of which 5 were waited for; matrix products, arithmetic and copies ran while one was open for 0% of the time, Pallas kernels for 31%

profile of v2, /device:TPU:0, one launch (start us, length us, event | category | flops | bytes accessed | tf_op | source)
XLA Modules:
  0.0 30.8 jit_solution(5616972633066918755)
XLA Ops:
  0.0 3.0 %collective-permute-start = (bf16[128,512]{1,0:T(8,128)(2,1)}, bf16[128,512]{1,0:T(8,128)(2,1)S(1)}, u32[]{:S(2)}, u32[]{:S(2)}) collective-permute-start(bf16[128,512]{1,0:T(8,128)(2,1)} %own.1), channel_id=1, source_target_pairs={{0,1},{1,0},{2,3},{3,2},{4,5},{5,4},{6,7},{7,6},{8,9},{9,8},{10,11... | collective-permute-start | bytes 393224 | tf_op jit(solution)/shard_map/ppermute | solution.py:332
  3.0 3.7 %collective-permute-start.2 = (bf16[128,512]{1,0:T(8,128)(2,1)}, bf16[128,512]{1,0:T(8,128)(2,1)S(1)}, u32[]{:S(2)}, u32[]{:S(2)}) collective-permute-start(bf16[128,512]{1,0:T(8,128)(2,1)} %own.1), channel_id=1, source_target_pairs={{2,4},{6,8},{10,12},{14,16},{18,20},{22,24},{26,28},{30,0},{4,2},{... | collective-permute-start | bytes 393224 | tf_op jit(solution)/shard_map/ppermute | solution.py:378
  6.7 3.2 %shard_map.91 = (bf16[128,768]{1,0:T(8,128)(2,1)S(1)}, f32[264,256]{1,0:T(8,128)S(1)}, f32[1,512]{1,0:T(1,128)S(1)}, bf16[512,768]{1,0:T(8,128)(2,1)S(1)}, bf16[...) custom-call(s32[2]{0:T(128)S(1)} %pad_add_fusion.where, ...), custom_call_target="tpu_custom_call" | custom-call | tf_op jit(solution)/shard_map/pallas_call | solution.py:305
  9.9 0.4 %shard_map.92 = (bf16[128,512]{1,0:T(8,128)(2,1)S(1)}, bf16[128,384]{1,0:T(8,128)(2,1)S(1)}) custom-call(bf16[128,512]{1,0:T(8,128)(2,1)S(1)} %collective-permute-done.feats, f32[1,512]{1,0:T(1,128)S(1)} %get-tuple-element.32.gain, bf16[512,768]{1,0:T(8,128)(2,1)S(1)} %get-tuple-element.33.w), custom_call_target="tpu_custom_call" | custom-call | tf_op jit(solution)/shard_map/pallas_call | solution.py:305
  10.3 0.6 %shard_map.95 = bf16[136,256]{1,0:T(8,128)(2,1)S(1)} custom-call(bf16[128,384]{1,0:T(8,128)(2,1)S(1)} %get-tuple-element.35.upper.qkv, bf16[4,128,256]{2,1,0:T(8,128)(2,1)S(1)} %get-tuple-element.37.both, f32[4,1]{1,0:T(4,128)S(1)} %get-tuple-element.38.factors, f32[128,1]{1,0:T(8,128)S(1)} %get-tuple-element.39.hidden, f32[264,256]{1,0:T(8,128)S(1)} %get-tuple-element.40.sums), custom_call_target="tpu_custom_call" | custom-call | tf_op jit(solution)/shard_map/pallas_call | solution.py:305
  11.5 0.6 %shard_map.94 = f32[136,256]{1,0:T(8,128)S(1)} custom-call(bf16[128,768]{1,0:T(8,128)(2,1)S(1)} %get-tuple-element.36.qkv.rest, bf16[4,128,256]{2,1,0:T(8,128)(2,1)S(1)} %get-tuple-element.37.both, f32[4,1]{1,0:T(4,128)S(1)} %get-tuple-element.38.factors, f32[128,1]{1,0:T(8,128)S(1)} %get-tuple-element.39.hidden, f32[264,256]{1,0:T(8,128)S(1)} %get-tuple-element.40.sums), custom_call_target="tpu_custom_call" | custom-call | tf_op jit(solution)/shard_map/pallas_call | solution.py:305
  12.0 0.3 %collective-permute-start.6 = (bf16[256,512]{1,0:T(8,128)(2,1)S(1)}, bf16[256,512]{1,0:T(8,128)(2,1)S(1)}, u32[]{:S(2)}, u32[]{:S(2)}) collective-permute-start(bf16[256,512]{1,0:T(8,128)(2,1)S(1)} %get-tuple-element.42), channel_id=1, source_target_pairs={{0,2},{2,0},{4,6},{6,4},{8,10},{10,8},{12,14},{14,12},{16,18},{18,... | collective-permute-start | bytes 786440 | tf_op jit(solution)/shard_map/ppermute | solution.py:339
  12.7 0.5 %collective-permute-start.4 = (bf16[136,256]{1,0:T(8,128)(2,1)S(1)}, bf16[136,256]{1,0:T(8,128)(2,1)S(1)}, u32[]{:S(2)}, u32[]{:S(2)}) collective-permute-start(bf16[136,256]{1,0:T(8,128)(2,1)S(1)} %fusion), channel_id=1, source_target_pairs={{0,4},{2,6},{4,0},{6,2},{8,12},{10,14},{12,8},{14,10},{16,20},{18,... | collective-permute-start | bytes 208904 | tf_op jit(solution)/shard_map/ppermute | solution.py:339
  13.1 2.8 %collective-permute-start.5 = (bf16[136,256]{1,0:T(8,128)(2,1)S(1)}, bf16[136,256]{1,0:T(8,128)(2,1)S(1)}, u32[]{:S(2)}, u32[]{:S(2)}) collective-permute-start(bf16[136,256]{1,0:T(8,128)(2,1)S(1)} %fusion), channel_id=1, source_target_pairs={{0,8},{2,10},{4,12},{6,14},{8,0},{10,2},{12,4},{14,6},{16,24},{18,... | collective-permute-start | bytes 208904 | tf_op jit(solution)/shard_map/ppermute | solution.py:339
  15.9 0.5 %collective-permute-start.8 = (bf16[128,512]{1,0:T(8,128)(2,1)S(1)}, bf16[128,512]{1,0:T(8,128)(2,1)S(1)}, u32[]{:S(2)}, u32[]{:S(2)}) collective-permute-start(bf16[128,512]{1,0:T(8,128)(2,1)S(1)} %collective-permute-done.2.far_own), channel_id=1, source_target_pairs={{0,1},{1,0},{2,3},{3,2},{4,5},{5,4},{6,7},{7,6},{8,9},{9,8},{10,11... | collective-permute-start | bytes 393224 | tf_op jit(solution)/shard_map/ppermute | solution.py:332
  16.4 0.6 %shard_map.96.kv = bf16[512,768]{1,0:T(8,128)(2,1)S(1)} custom-call(bf16[256,512]{1,0:T(8,128)(2,1)S(1)} %collective-permute-done.6.near, f32[1,512]{1,0:T(1,128)S(1)} %get-tuple-element.32.gain, bf16[512,768]{1,0:T(8,128)(2,1)S(1)} %get-tuple-element.33.w, bf16[128,768]{1,0:T(8,128)(2,1)S(1)} %get-tuple-element.43.own, ...), custom_call_target="tpu_custom_call" | custom-call | tf_op jit(solution)/shard_map/pallas_call | solution.py:305
  17.0 0.6 %shard_map.97.phi_q = bf16[4,256,256]{2,1,0:T(8,128)(2,1)S(1)} custom-call(bf16[512,768]{1,0:T(8,128)(2,1)S(1)} %shard_map.96.kv, bf16[4,128,256]{2,1,0:T(8,128)(2,1)S(1)} %get-tuple-element.37.both, f32[4,1]{1,0:T(4,128)S(1)} %get-tuple-element.38.factors), custom_call_target="tpu_custom_call" | custom-call | tf_op jit(solution)/shard_map/pallas_call | solution.py:305
  17.7 0.7 %collective-permute-done.3 = bf16[136,256]{1,0:T(8,128)(2,1)S(1)} collective-permute-done((bf16[136,256]{1,0:T(8,128)(2,1)S(1)}, bf16[136,256]{1,0:T(8,128)(2,1)S(1)}, u32[]{:S(2)}, u32[]{:S(2)}) %collective-permute-start.3) | collective-permute-done | bytes 69664 | tf_op jit(solution)/shard_map/ppermute | solution.py:339
  18.5 1.7 %collective-permute-start.7 = (bf16[136,256]{1,0:T(8,128)(2,1)S(1)}, bf16[136,256]{1,0:T(8,128)(2,1)S(1)}, u32[]{:S(2)}, u32[]{:S(2)}) collective-permute-start(bf16[136,256]{1,0:T(8,128)(2,1)S(1)} %fusion.1), channel_id=1, source_target_pairs={{0,16},{2,18},{4,20},{6,22},{8,24},{10,26},{12,28},{14,30},{16,0},... | collective-permute-start | bytes 208904 | tf_op jit(solution)/shard_map/ppermute | solution.py:339
  20.2 0.7 %collective-permute-done.8.far_rest = bf16[128,512]{1,0:T(8,128)(2,1)S(1)} collective-permute-done((bf16[128,512]{1,0:T(8,128)(2,1)S(1)}, bf16[128,512]{1,0:T(8,128)(2,1)S(1)}, u32[]{:S(2)}, u32[]{:S(2)}) %collective-permute-start.8) | collective-permute-done | bytes 131104 | tf_op jit(solution)/shard_map/ppermute | solution.py:332
  20.9 0.6 %shard_map.98.far = bf16[256,768]{1,0:T(8,128)(2,1)S(1)} custom-call(bf16[128,512]{1,0:T(8,128)(2,1)S(1)} %collective-permute-done.2.far_own, bf16[128,512]{1,0:T(8,128)(2,1)S(1)} %collective-permute-done.8.far_rest, f32[1,512]{1,0:T(1,128)S(1)} %get-tuple-element.32.gain, bf16[512,768]{1,0:T(8,128)(2,1)S(1)} %get-tuple-element.33.w), custom_call_target="tpu_custom_call" | custom-call | tf_op jit(solution)/shard_map/pallas_call | solution.py:305
  21.5 1.2 %shard_map.99.local = f32[256,128]{1,0:T(8,128)S(1)} custom-call(bf16[512,768]{1,0:T(8,128)(2,1)S(1)} %shard_map.96.kv, bf16[256,768]{1,0:T(8,128)(2,1)S(1)} %shard_map.98.far, f32[2,768]{1,0:T(2,128)S(1)} %get-tuple-element.50.bias), custom_call_target="tpu_custom_call" | custom-call | tf_op jit(solution)/shard_map/pallas_call | solution.py:305
  22.7 1.2 %shard_map.100.local = f32[256,128]{1,0:T(8,128)S(1)} custom-call(bf16[512,768]{1,0:T(8,128)(2,1)S(1)} %shard_map.96.kv, bf16[256,768]{1,0:T(8,128)(2,1)S(1)} %shard_map.98.far, f32[2,768]{1,0:T(2,128)S(1)} %get-tuple-element.50.bias), custom_call_target="tpu_custom_call" | custom-call | tf_op jit(solution)/shard_map/pallas_call | solution.py:305
  24.1 0.3 shard_map.101
  24.4 0.9 %collective-permute-done.9.sums = bf16[136,256]{1,0:T(8,128)(2,1)S(1)} collective-permute-done((bf16[136,256]{1,0:T(8,128)(2,1)S(1)}, bf16[136,256]{1,0:T(8,128)(2,1)S(1)}, u32[]{:S(2)}, u32[]{:S(2)}) %collective-permute-start.9) | collective-permute-done | bytes 69664 | tf_op jit(solution)/shard_map/ppermute | solution.py:339
  25.3 0.3 shard_map.102
  25.6 0.7 %collective-permute-start.10 = (bf16[128,256]{1,0:T(8,128)(2,1)S(1)}, bf16[128,256]{1,0:T(8,128)(2,1)S(1)}, u32[]{:S(2)}, u32[]{:S(2)}) collective-permute-start(bf16[128,256]{1,0:T(8,128)(2,1)S(1)} %bitcast.4), channel_id=1, source_target_pairs={{0,1},{1,0},{2,3},{3,2},{4,5},{5,4},{6,7},{7,6},{8,9},{9,8},{10,11... | collective-permute-start | bytes 196616 | tf_op jit(solution)/shard_map/ppermute | solution.py:332
  26.5 3.4 %collective-permute-done.10.refs_0_ = bf16[128,256]{1,0:T(8,128)(2,1)S(1)} collective-permute-done((bf16[128,256]{1,0:T(8,128)(2,1)S(1)}, bf16[128,256]{1,0:T(8,128)(2,1)S(1)}, u32[]{:S(2)}, u32[]{:S(2)}) %collective-permute-start.10) | collective-permute-done | bytes 65568 | tf_op jit(solution)/shard_map/ppermute | solution.py:332
  29.9 0.8 %shard_map.104 = bf16[128,512]{1,0:T(8,128)(2,1)} custom-call(f32[128,512]{1,0:T(8,128)S(1)} %shard_map.103.first, bf16[128,256]{1,0:T(8,128)(2,1)S(1)} %collective-permute-done.10.refs_0_, bf16[512,512]{1,0:T(8,128)(2,1)S(1)} %get-tuple-element.57.w.refs_1_), custom_call_target="tpu_custom_call" | custom-call | tf_op jit(solution)/shard_map/pallas_call | solution.py:305
  (18 shorter events, 1.4 us)
Async XLA Ops:
  0.0 9.9 %collective-permute-start = (bf16[128,512]{1,0:T(8,128)(2,1)}, bf16[128,512]{1,0:T(8,128)(2,1)S(1)}, u32[]{:S(2)}, u32[]{:S(2)}) collective-permute-start(bf16[128,512]{1,0:T(8,128)(2,1)} %own.1), channel_id=1, source_target_pairs={{0,1},{1,0},{2,3},{3,2},{4,5},{5,4},{6,7},{7,6},{8,9},{9,8},{10,11... | collective-permute-start | bytes 393224 | tf_op jit(solution)/shard_map/ppermute | solution.py:332
  3.0 9.4 %collective-permute-start.2 = (bf16[128,512]{1,0:T(8,128)(2,1)}, bf16[128,512]{1,0:T(8,128)(2,1)S(1)}, u32[]{:S(2)}, u32[]{:S(2)}) collective-permute-start(bf16[128,512]{1,0:T(8,128)(2,1)} %own.1), channel_id=1, source_target_pairs={{2,4},{6,8},{10,12},{14,16},{18,20},{22,24},{26,28},{30,0},{4,2},{... | collective-permute-start | bytes 393224 | tf_op jit(solution)/shard_map/ppermute | solution.py:378
  10.3 0.9 %copy-start = (bf16[128,512]{1,0:T(8,128)(2,1)S(1)}, bf16[128,512]{1,0:T(8,128)(2,1)}, u32[]{:S(2)}) copy-start(bf16[128,512]{1,0:T(8,128)(2,1)} %own.1) | copy-start | bytes 393220
  10.9 1.4 %collective-permute-start.1 = (bf16[136,256]{1,0:T(8,128)(2,1)S(1)}, bf16[136,256]{1,0:T(8,128)(2,1)S(1)}, u32[]{:S(2)}, u32[]{:S(2)}) collective-permute-start(bf16[136,256]{1,0:T(8,128)(2,1)S(1)} %shard_map.95), channel_id=1, source_target_pairs={{0,2},{2,0},{4,6},{6,4},{8,10},{10,8},{12,14},{14,12},{16,18},{18,... | collective-permute-start | bytes 208904 | tf_op jit(solution)/shard_map/ppermute | solution.py:339
  12.0 4.4 %collective-permute-start.6 = (bf16[256,512]{1,0:T(8,128)(2,1)S(1)}, bf16[256,512]{1,0:T(8,128)(2,1)S(1)}, u32[]{:S(2)}, u32[]{:S(2)}) collective-permute-start(bf16[256,512]{1,0:T(8,128)(2,1)S(1)} %get-tuple-element.42), channel_id=1, source_target_pairs={{0,2},{2,0},{4,6},{6,4},{8,10},{10,8},{12,14},{14,12},{16,18},{18,... | collective-permute-start | bytes 786440 | tf_op jit(solution)/shard_map/ppermute | solution.py:339
  12.4 6.0 %collective-permute-start.3 = (bf16[136,256]{1,0:T(8,128)(2,1)S(1)}, bf16[136,256]{1,0:T(8,128)(2,1)S(1)}, u32[]{:S(2)}, u32[]{:S(2)}) collective-permute-start(bf16[136,256]{1,0:T(8,128)(2,1)S(1)} %fusion), channel_id=1, source_target_pairs={{0,12},{2,14},{4,8},{6,10},{8,4},{10,6},{12,0},{14,2},{16,28},{18,... | collective-permute-start | bytes 208904 | tf_op jit(solution)/shard_map/ppermute | solution.py:339
  12.7 5.8 %collective-permute-start.4 = (bf16[136,256]{1,0:T(8,128)(2,1)S(1)}, bf16[136,256]{1,0:T(8,128)(2,1)S(1)}, u32[]{:S(2)}, u32[]{:S(2)}) collective-permute-start(bf16[136,256]{1,0:T(8,128)(2,1)S(1)} %fusion), channel_id=1, source_target_pairs={{0,4},{2,6},{4,0},{6,2},{8,12},{10,14},{12,8},{14,10},{16,20},{18,... | collective-permute-start | bytes 208904 | tf_op jit(solution)/shard_map/ppermute | solution.py:339
  13.1 5.3 %collective-permute-start.5 = (bf16[136,256]{1,0:T(8,128)(2,1)S(1)}, bf16[136,256]{1,0:T(8,128)(2,1)S(1)}, u32[]{:S(2)}, u32[]{:S(2)}) collective-permute-start(bf16[136,256]{1,0:T(8,128)(2,1)S(1)} %fusion), channel_id=1, source_target_pairs={{0,8},{2,10},{4,12},{6,14},{8,0},{10,2},{12,4},{14,6},{16,24},{18,... | collective-permute-start | bytes 208904 | tf_op jit(solution)/shard_map/ppermute | solution.py:339
  15.9 5.0 %collective-permute-start.8 = (bf16[128,512]{1,0:T(8,128)(2,1)S(1)}, bf16[128,512]{1,0:T(8,128)(2,1)S(1)}, u32[]{:S(2)}, u32[]{:S(2)}) collective-permute-start(bf16[128,512]{1,0:T(8,128)(2,1)S(1)} %collective-permute-done.2.far_own), channel_id=1, source_target_pairs={{0,1},{1,0},{2,3},{3,2},{4,5},{5,4},{6,7},{7,6},{8,9},{9,8},{10,11... | collective-permute-start | bytes 393224 | tf_op jit(solution)/shard_map/ppermute | solution.py:332
  18.5 5.4 %collective-permute-start.7 = (bf16[136,256]{1,0:T(8,128)(2,1)S(1)}, bf16[136,256]{1,0:T(8,128)(2,1)S(1)}, u32[]{:S(2)}, u32[]{:S(2)}) collective-permute-start(bf16[136,256]{1,0:T(8,128)(2,1)S(1)} %fusion.1), channel_id=1, source_target_pairs={{0,16},{2,18},{4,20},{6,22},{8,24},{10,26},{12,28},{14,30},{16,0},... | collective-permute-start | bytes 208904 | tf_op jit(solution)/shard_map/ppermute | solution.py:339
  24.0 1.3 %collective-permute-start.9 = (bf16[136,256]{1,0:T(8,128)(2,1)S(1)}, bf16[136,256]{1,0:T(8,128)(2,1)S(1)}, u32[]{:S(2)}, u32[]{:S(2)}) collective-permute-start(bf16[136,256]{1,0:T(8,128)(2,1)S(1)} %add_convert_fusion.sums), channel_id=1, source_target_pairs={{0,2},{2,0},{4,6},{6,4},{8,10},{10,8},{12,14},{14,12},{16,18},{18,... | collective-permute-start | bytes 208904 | tf_op jit(solution)/shard_map/ppermute | solution.py:339
  25.6 4.3 %collective-permute-start.10 = (bf16[128,256]{1,0:T(8,128)(2,1)S(1)}, bf16[128,256]{1,0:T(8,128)(2,1)S(1)}, u32[]{:S(2)}, u32[]{:S(2)}) collective-permute-start(bf16[128,256]{1,0:T(8,128)(2,1)S(1)} %bitcast.4), channel_id=1, source_target_pairs={{0,1},{1,0},{2,3},{3,2},{4,5},{5,4},{6,7},{7,6},{8,9},{9,8},{10,11... | collective-permute-start | bytes 196616 | tf_op jit(solution)/shard_map/ppermute | solution.py:332

commit v3 on v0

--- a/solution.py
+++ b/solution.py
@@ -257,7 +257,7 @@
         keep[:, :start] = before[0][...]
         send[:, :, :start] = before[1][...]
     split = sums.shape[1] // 2
-    totals = sums[len(chosen) * head_dim :, :].astype(F32)
+    totals = sums[...].astype(F32)[len(chosen) * head_dim :]
     for i, h in enumerate(chosen):
         cols = slice(i * head_dim, (i + 1) * head_dim)
         low, high = phi_q[h, :, :split], phi_q[h, :, split:]
@@ -411,7 +411,7 @@
         phi_kernel, [((heads, rows, count), BF16)], [VM] * 3, (kv, both, factors), limit
     )
     sent = keep.astype(BF16)
-    first, second, third = [crossed(sent, bit) for bit in (6, 4, 2)]
+    first, second, third = [crossed(sent, bit) for bit in (6, 2, 4)]
     first, second, third, kv, phi_q = lax.optimization_barrier((first, second, third, kv, phi_q))
     keep = keep + first.astype(F32) + second.astype(F32) + third.astype(F32)
     far_rest = gathered(far_own)

time: 31.6 us -> 30.8 us (0.975)
  waiting for transfers between devices: 7.62 us -> 5.95 us
  starting transfers between devices: 12.9 us -> 13.8 us
    ppermute x7, waiting for transfers between devices: 3.24 us -> 1.7 us  [crossed(): return lax.ppermute(array, 'dom', [(i, i ^ bit) for i in range(doms)])]
    ppermute x7, starting transfers between devices: 5.16 us -> 5.93 us  [crossed(): return lax.ppermute(array, 'dom', [(i, i ^ bit) for i in range(doms)])]
  transfers between devices with their start and end apart: 11 -> 11, of which waited for: 7 -> 5; matrix products, arithmetic and copies ran while one was open for 0% -> 0% of each run, Pallas kernels for 30% -> 31%
where the time goes in v3:
time: 30.8 us; the launch traced here: 30.7 us
  starting transfers between devices  13.8 us (45%)
  Pallas kernels  10.6 us (34%)
  waiting for transfers between devices  5.95 us (19%)
    pallas_call x13, Pallas kernels, call(): pl.pallas_call(body, out_shape=shapes, in_specs=specs, out_specs=(VM,) *...  10.6 us
    ppermute x7, starting transfers between devices, crossed(): return lax.ppermute(array, 'dom', [(i, i ^ bit) for i in range(doms)])  5.93 us
    ppermute x3, waiting for transfers between devices, shifted(): lax.ppermute(array, 'head', [(i, (i + step) % groups) for i in range(grou...  4.25 us
    ppermute x3, starting transfers between devices, shifted(): lax.ppermute(array, 'head', [(i, (i + step) % groups) for i in range(grou...  4.2 us
    ppermute x1, starting transfers between devices, shards(): lax.ppermute(node_feats, 'dom', pairs + [(b, a) for a, b in pairs])  3.69 us
    ppermute x7, waiting for transfers between devices, crossed(): return lax.ppermute(array, 'dom', [(i, i ^ bit) for i in range(doms)])  1.7 us
  transfers between devices with their start and end apart: 11, of which 5 were waited for; matrix products, arithmetic and copies ran while one was open for 0% of the time, Pallas kernels for 31%

profile of v3, /device:TPU:0, one launch (start us, length us, event | category | flops | bytes accessed | tf_op | source)
XLA Modules:
  0.0 30.7 jit_solution(13898755446752033449)
XLA Ops:
  0.0 3.0 %collective-permute-start = (bf16[128,512]{1,0:T(8,128)(2,1)}, bf16[128,512]{1,0:T(8,128)(2,1)S(1)}, u32[]{:S(2)}, u32[]{:S(2)}) collective-permute-start(bf16[128,512]{1,0:T(8,128)(2,1)} %own.1), channel_id=1, source_target_pairs={{0,1},{1,0},{2,3},{3,2},{4,5},{5,4},{6,7},{7,6},{8,9},{9,8},{10,11... | collective-permute-start | bytes 393224 | tf_op jit(solution)/shard_map/ppermute | solution.py:318
  3.0 3.7 %collective-permute-start.2 = (bf16[128,512]{1,0:T(8,128)(2,1)}, bf16[128,512]{1,0:T(8,128)(2,1)S(1)}, u32[]{:S(2)}, u32[]{:S(2)}) collective-permute-start(bf16[128,512]{1,0:T(8,128)(2,1)} %own.1), channel_id=1, source_target_pairs={{2,4},{6,8},{10,12},{14,16},{18,20},{22,24},{26,28},{30,0},{4,2},{... | collective-permute-start | bytes 393224 | tf_op jit(solution)/shard_map/ppermute | solution.py:364
  6.7 3.2 %shard_map.91 = (bf16[128,768]{1,0:T(8,128)(2,1)S(1)}, f32[264,256]{1,0:T(8,128)S(1)}, f32[1,512]{1,0:T(1,128)S(1)}, bf16[512,768]{1,0:T(8,128)(2,1)S(1)}, bf16[...) custom-call(s32[2]{0:T(128)S(1)} %pad_add_fusion.where, ...), custom_call_target="tpu_custom_call" | custom-call | tf_op jit(solution)/shard_map/pallas_call | solution.py:291
  9.9 0.4 %shard_map.92 = (bf16[128,768]{1,0:T(8,128)(2,1)S(1)}, bf16[256,512]{1,0:T(8,128)(2,1)S(1)}) custom-call(bf16[128,512]{1,0:T(8,128)(2,1)S(1)} %collective-permute-done.feats, bf16[128,512]{1,0:T(8,128)(2,1)S(1)} %copy-done, f32[1,512]{1,0:T(1,128)S(1)} %get-tuple-element.30.gain, bf16[512,768]{1,0:T(8,128)(2,1)S(1)} %get-tuple-element.31.w), custom_call_target="tpu_custom_call" | custom-call | tf_op jit(solution)/shard_map/pallas_call | solution.py:291
  10.4 0.6 %shard_map.94 = bf16[136,256]{1,0:T(8,128)(2,1)S(1)} custom-call(bf16[128,768]{1,0:T(8,128)(2,1)S(1)} %get-tuple-element.32.qkv.rest, bf16[4,128,256]{2,1,0:T(8,128)(2,1)S(1)} %get-tuple-element.33.both, f32[4,1]{1,0:T(4,128)S(1)} %get-tuple-element.34.factors, f32[128,1]{1,0:T(8,128)S(1)} %get-tuple-element.35.hidden, f32[264,256]{1,0:T(8,128)S(1)} %get-tuple-element.36.sums), custom_call_target="tpu_custom_call" | custom-call | tf_op jit(solution)/shard_map/pallas_call | solution.py:291
  11.0 0.6 %shard_map.93 = f32[136,256]{1,0:T(8,128)S(1)} custom-call(bf16[128,768]{1,0:T(8,128)(2,1)S(1)} %get-tuple-element.32.qkv.rest, bf16[4,128,256]{2,1,0:T(8,128)(2,1)S(1)} %get-tuple-element.33.both, f32[4,1]{1,0:T(4,128)S(1)} %get-tuple-element.34.factors, f32[128,1]{1,0:T(8,128)S(1)} %get-tuple-element.35.hidden, f32[264,256]{1,0:T(8,128)S(1)} %get-tuple-element.36.sums), custom_call_target="tpu_custom_call" | custom-call | tf_op jit(solution)/shard_map/pallas_call | solution.py:291
  11.6 0.6 %collective-permute-start.6 = (bf16[256,512]{1,0:T(8,128)(2,1)S(1)}, bf16[256,512]{1,0:T(8,128)(2,1)S(1)}, u32[]{:S(2)}, u32[]{:S(2)}) collective-permute-start(bf16[256,512]{1,0:T(8,128)(2,1)S(1)} %get-tuple-element.38), channel_id=1, source_target_pairs={{0,2},{2,0},{4,6},{6,4},{8,10},{10,8},{12,14},{14,12},{16,18},{18,... | collective-permute-start | bytes 786440 | tf_op jit(solution)/shard_map/ppermute | solution.py:325
  12.5 0.5 %collective-permute-start.4 = (bf16[136,256]{1,0:T(8,128)(2,1)S(1)}, bf16[136,256]{1,0:T(8,128)(2,1)S(1)}, u32[]{:S(2)}, u32[]{:S(2)}) collective-permute-start(bf16[136,256]{1,0:T(8,128)(2,1)S(1)} %fusion), channel_id=1, source_target_pairs={{0,4},{2,6},{4,0},{6,2},{8,12},{10,14},{12,8},{14,10},{16,20},{18,... | collective-permute-start | bytes 208904 | tf_op jit(solution)/shard_map/ppermute | solution.py:325
  13.0 2.9 %collective-permute-start.5 = (bf16[136,256]{1,0:T(8,128)(2,1)S(1)}, bf16[136,256]{1,0:T(8,128)(2,1)S(1)}, u32[]{:S(2)}, u32[]{:S(2)}) collective-permute-start(bf16[136,256]{1,0:T(8,128)(2,1)S(1)} %fusion), channel_id=1, source_target_pairs={{0,8},{2,10},{4,12},{6,14},{8,0},{10,2},{12,4},{14,6},{16,24},{18,... | collective-permute-start | bytes 208904 | tf_op jit(solution)/shard_map/ppermute | solution.py:325
  15.9 0.5 %collective-permute-start.8 = (bf16[128,512]{1,0:T(8,128)(2,1)S(1)}, bf16[128,512]{1,0:T(8,128)(2,1)S(1)}, u32[]{:S(2)}, u32[]{:S(2)}) collective-permute-start(bf16[128,512]{1,0:T(8,128)(2,1)S(1)} %collective-permute-done.2.far_own), channel_id=1, source_target_pairs={{0,1},{1,0},{2,3},{3,2},{4,5},{5,4},{6,7},{7,6},{8,9},{9,8},{10,11... | collective-permute-start | bytes 393224 | tf_op jit(solution)/shard_map/ppermute | solution.py:318
  16.4 0.6 %shard_map.95.kv = bf16[512,768]{1,0:T(8,128)(2,1)S(1)} custom-call(bf16[256,512]{1,0:T(8,128)(2,1)S(1)} %collective-permute-done.6.near, f32[1,512]{1,0:T(1,128)S(1)} %get-tuple-element.30.gain, bf16[512,768]{1,0:T(8,128)(2,1)S(1)} %get-tuple-element.31.w, bf16[128,768]{1,0:T(8,128)(2,1)S(1)} %get-tuple-element.39.own, ...), custom_call_target="tpu_custom_call" | custom-call | tf_op jit(solution)/shard_map/pallas_call | solution.py:291
  17.0 0.6 %shard_map.96.phi_q = bf16[4,256,256]{2,1,0:T(8,128)(2,1)S(1)} custom-call(bf16[512,768]{1,0:T(8,128)(2,1)S(1)} %shard_map.95.kv, bf16[4,128,256]{2,1,0:T(8,128)(2,1)S(1)} %get-tuple-element.33.both, f32[4,1]{1,0:T(4,128)S(1)} %get-tuple-element.34.factors), custom_call_target="tpu_custom_call" | custom-call | tf_op jit(solution)/shard_map/pallas_call | solution.py:291
  17.6 0.6 %collective-permute-done.3 = bf16[136,256]{1,0:T(8,128)(2,1)S(1)} collective-permute-done((bf16[136,256]{1,0:T(8,128)(2,1)S(1)}, bf16[136,256]{1,0:T(8,128)(2,1)S(1)}, u32[]{:S(2)}, u32[]{:S(2)}) %collective-permute-start.3) | collective-permute-done | bytes 69664 | tf_op jit(solution)/shard_map/ppermute | solution.py:325
  18.3 1.7 %collective-permute-start.7 = (bf16[136,256]{1,0:T(8,128)(2,1)S(1)}, bf16[136,256]{1,0:T(8,128)(2,1)S(1)}, u32[]{:S(2)}, u32[]{:S(2)}) collective-permute-start(bf16[136,256]{1,0:T(8,128)(2,1)S(1)} %fusion.1), channel_id=1, source_target_pairs={{0,16},{2,18},{4,20},{6,22},{8,24},{10,26},{12,28},{14,30},{16,0},... | collective-permute-start | bytes 208904 | tf_op jit(solution)/shard_map/ppermute | solution.py:325
  20.0 0.8 %collective-permute-done.8.far_rest = bf16[128,512]{1,0:T(8,128)(2,1)S(1)} collective-permute-done((bf16[128,512]{1,0:T(8,128)(2,1)S(1)}, bf16[128,512]{1,0:T(8,128)(2,1)S(1)}, u32[]{:S(2)}, u32[]{:S(2)}) %collective-permute-start.8) | collective-permute-done | bytes 131104 | tf_op jit(solution)/shard_map/ppermute | solution.py:318
  20.8 0.6 %shard_map.97.far = bf16[256,768]{1,0:T(8,128)(2,1)S(1)} custom-call(bf16[128,512]{1,0:T(8,128)(2,1)S(1)} %collective-permute-done.2.far_own, bf16[128,512]{1,0:T(8,128)(2,1)S(1)} %collective-permute-done.8.far_rest, f32[1,512]{1,0:T(1,128)S(1)} %get-tuple-element.30.gain, bf16[512,768]{1,0:T(8,128)(2,1)S(1)} %get-tuple-element.31.w), custom_call_target="tpu_custom_call" | custom-call | tf_op jit(solution)/shard_map/pallas_call | solution.py:291
  21.4 1.2 %shard_map.98.local = f32[256,128]{1,0:T(8,128)S(1)} custom-call(bf16[512,768]{1,0:T(8,128)(2,1)S(1)} %shard_map.95.kv, bf16[256,768]{1,0:T(8,128)(2,1)S(1)} %shard_map.97.far, f32[2,768]{1,0:T(2,128)S(1)} %get-tuple-element.46.bias), custom_call_target="tpu_custom_call" | custom-call | tf_op jit(solution)/shard_map/pallas_call | solution.py:291
  22.6 1.2 %shard_map.99.local = f32[256,128]{1,0:T(8,128)S(1)} custom-call(bf16[512,768]{1,0:T(8,128)(2,1)S(1)} %shard_map.95.kv, bf16[256,768]{1,0:T(8,128)(2,1)S(1)} %shard_map.97.far, f32[2,768]{1,0:T(2,128)S(1)} %get-tuple-element.46.bias), custom_call_target="tpu_custom_call" | custom-call | tf_op jit(solution)/shard_map/pallas_call | solution.py:291
  24.0 0.3 shard_map.100
  24.3 0.9 %collective-permute-done.9.sums = bf16[136,256]{1,0:T(8,128)(2,1)S(1)} collective-permute-done((bf16[136,256]{1,0:T(8,128)(2,1)S(1)}, bf16[136,256]{1,0:T(8,128)(2,1)S(1)}, u32[]{:S(2)}, u32[]{:S(2)}) %collective-permute-start.9) | collective-permute-done | bytes 69664 | tf_op jit(solution)/shard_map/ppermute | solution.py:325
  25.2 0.3 shard_map.101
  25.5 0.7 %collective-permute-start.10 = (bf16[128,256]{1,0:T(8,128)(2,1)S(1)}, bf16[128,256]{1,0:T(8,128)(2,1)S(1)}, u32[]{:S(2)}, u32[]{:S(2)}) collective-permute-start(bf16[128,256]{1,0:T(8,128)(2,1)S(1)} %bitcast.4), channel_id=1, source_target_pairs={{0,1},{1,0},{2,3},{3,2},{4,5},{5,4},{6,7},{7,6},{8,9},{9,8},{10,11... | collective-permute-start | bytes 196616 | tf_op jit(solution)/shard_map/ppermute | solution.py:318
  26.4 3.4 %collective-permute-done.10.refs_0_ = bf16[128,256]{1,0:T(8,128)(2,1)S(1)} collective-permute-done((bf16[128,256]{1,0:T(8,128)(2,1)S(1)}, bf16[128,256]{1,0:T(8,128)(2,1)S(1)}, u32[]{:S(2)}, u32[]{:S(2)}) %collective-permute-start.10) | collective-permute-done | bytes 65568 | tf_op jit(solution)/shard_map/ppermute | solution.py:318
  29.9 0.8 %shard_map.103 = bf16[128,512]{1,0:T(8,128)(2,1)} custom-call(f32[128,512]{1,0:T(8,128)S(1)} %shard_map.102.first, bf16[128,256]{1,0:T(8,128)(2,1)S(1)} %collective-permute-done.10.refs_0_, bf16[512,512]{1,0:T(8,128)(2,1)S(1)} %get-tuple-element.53.w.refs_1_), custom_call_target="tpu_custom_call" | custom-call | tf_op jit(solution)/shard_map/pallas_call | solution.py:291
  (17 shorter events, 0.9 us)
Async XLA Ops:
  0.0 9.9 %collective-permute-start = (bf16[128,512]{1,0:T(8,128)(2,1)}, bf16[128,512]{1,0:T(8,128)(2,1)S(1)}, u32[]{:S(2)}, u32[]{:S(2)}) collective-permute-start(bf16[128,512]{1,0:T(8,128)(2,1)} %own.1), channel_id=1, source_target_pairs={{0,1},{1,0},{2,3},{3,2},{4,5},{5,4},{6,7},{7,6},{8,9},{9,8},{10,11... | collective-permute-start | bytes 393224 | tf_op jit(solution)/shard_map/ppermute | solution.py:318
  3.0 9.2 %collective-permute-start.2 = (bf16[128,512]{1,0:T(8,128)(2,1)}, bf16[128,512]{1,0:T(8,128)(2,1)S(1)}, u32[]{:S(2)}, u32[]{:S(2)}) collective-permute-start(bf16[128,512]{1,0:T(8,128)(2,1)} %own.1), channel_id=1, source_target_pairs={{2,4},{6,8},{10,12},{14,16},{18,20},{22,24},{26,28},{30,0},{4,2},{... | collective-permute-start | bytes 393224 | tf_op jit(solution)/shard_map/ppermute | solution.py:364
  6.7 3.2 %copy-start = (bf16[128,512]{1,0:T(8,128)(2,1)S(1)}, bf16[128,512]{1,0:T(8,128)(2,1)}, u32[]{:S(2)}) copy-start(bf16[128,512]{1,0:T(8,128)(2,1)} %own.1) | copy-start | bytes 393220
  11.0 1.3 %collective-permute-start.1 = (bf16[136,256]{1,0:T(8,128)(2,1)S(1)}, bf16[136,256]{1,0:T(8,128)(2,1)S(1)}, u32[]{:S(2)}, u32[]{:S(2)}) collective-permute-start(bf16[136,256]{1,0:T(8,128)(2,1)S(1)} %shard_map.94), channel_id=1, source_target_pairs={{0,2},{2,0},{4,6},{6,4},{8,10},{10,8},{12,14},{14,12},{16,18},{18,... | collective-permute-start | bytes 208904 | tf_op jit(solution)/shard_map/ppermute | solution.py:325
  11.6 4.8 %collective-permute-start.6 = (bf16[256,512]{1,0:T(8,128)(2,1)S(1)}, bf16[256,512]{1,0:T(8,128)(2,1)S(1)}, u32[]{:S(2)}, u32[]{:S(2)}) collective-permute-start(bf16[256,512]{1,0:T(8,128)(2,1)S(1)} %get-tuple-element.38), channel_id=1, source_target_pairs={{0,2},{2,0},{4,6},{6,4},{8,10},{10,8},{12,14},{14,12},{16,18},{18,... | collective-permute-start | bytes 786440 | tf_op jit(solution)/shard_map/ppermute | solution.py:325
  12.3 6.0 %collective-permute-start.3 = (bf16[136,256]{1,0:T(8,128)(2,1)S(1)}, bf16[136,256]{1,0:T(8,128)(2,1)S(1)}, u32[]{:S(2)}, u32[]{:S(2)}) collective-permute-start(bf16[136,256]{1,0:T(8,128)(2,1)S(1)} %fusion), channel_id=1, source_target_pairs={{0,12},{2,14},{4,8},{6,10},{8,4},{10,6},{12,0},{14,2},{16,28},{18,... | collective-permute-start | bytes 208904 | tf_op jit(solution)/shard_map/ppermute | solution.py:325
  12.5 5.8 %collective-permute-start.4 = (bf16[136,256]{1,0:T(8,128)(2,1)S(1)}, bf16[136,256]{1,0:T(8,128)(2,1)S(1)}, u32[]{:S(2)}, u32[]{:S(2)}) collective-permute-start(bf16[136,256]{1,0:T(8,128)(2,1)S(1)} %fusion), channel_id=1, source_target_pairs={{0,4},{2,6},{4,0},{6,2},{8,12},{10,14},{12,8},{14,10},{16,20},{18,... | collective-permute-start | bytes 208904 | tf_op jit(solution)/shard_map/ppermute | solution.py:325
  13.0 5.3 %collective-permute-start.5 = (bf16[136,256]{1,0:T(8,128)(2,1)S(1)}, bf16[136,256]{1,0:T(8,128)(2,1)S(1)}, u32[]{:S(2)}, u32[]{:S(2)}) collective-permute-start(bf16[136,256]{1,0:T(8,128)(2,1)S(1)} %fusion), channel_id=1, source_target_pairs={{0,8},{2,10},{4,12},{6,14},{8,0},{10,2},{12,4},{14,6},{16,24},{18,... | collective-permute-start | bytes 208904 | tf_op jit(solution)/shard_map/ppermute | solution.py:325
  15.9 5.0 %collective-permute-start.8 = (bf16[128,512]{1,0:T(8,128)(2,1)S(1)}, bf16[128,512]{1,0:T(8,128)(2,1)S(1)}, u32[]{:S(2)}, u32[]{:S(2)}) collective-permute-start(bf16[128,512]{1,0:T(8,128)(2,1)S(1)} %collective-permute-done.2.far_own), channel_id=1, source_target_pairs={{0,1},{1,0},{2,3},{3,2},{4,5},{5,4},{6,7},{7,6},{8,9},{9,8},{10,11... | collective-permute-start | bytes 393224 | tf_op jit(solution)/shard_map/ppermute | solution.py:318
  18.3 5.5 %collective-permute-start.7 = (bf16[136,256]{1,0:T(8,128)(2,1)S(1)}, bf16[136,256]{1,0:T(8,128)(2,1)S(1)}, u32[]{:S(2)}, u32[]{:S(2)}) collective-permute-start(bf16[136,256]{1,0:T(8,128)(2,1)S(1)} %fusion.1), channel_id=1, source_target_pairs={{0,16},{2,18},{4,20},{6,22},{8,24},{10,26},{12,28},{14,30},{16,0},... | collective-permute-start | bytes 208904 | tf_op jit(solution)/shard_map/ppermute | solution.py:325
  23.9 1.3 %collective-permute-start.9 = (bf16[136,256]{1,0:T(8,128)(2,1)S(1)}, bf16[136,256]{1,0:T(8,128)(2,1)S(1)}, u32[]{:S(2)}, u32[]{:S(2)}) collective-permute-start(bf16[136,256]{1,0:T(8,128)(2,1)S(1)} %add_convert_fusion.sums), channel_id=1, source_target_pairs={{0,2},{2,0},{4,6},{6,4},{8,10},{10,8},{12,14},{14,12},{16,18},{18,... | collective-permute-start | bytes 208904 | tf_op jit(solution)/shard_map/ppermute | solution.py:325
  25.5 4.3 %collective-permute-start.10 = (bf16[128,256]{1,0:T(8,128)(2,1)S(1)}, bf16[128,256]{1,0:T(8,128)(2,1)S(1)}, u32[]{:S(2)}, u32[]{:S(2)}) collective-permute-start(bf16[128,256]{1,0:T(8,128)(2,1)S(1)} %bitcast.4), channel_id=1, source_target_pairs={{0,1},{1,0},{2,3},{3,2},{4,5},{5,4},{6,7},{7,6},{8,9},{9,8},{10,11... | collective-permute-start | bytes 196616 | tf_op jit(solution)/shard_map/ppermute | solution.py:318

commit v4 on v3

--- a/solution.py
+++ b/solution.py
@@ -278,21 +278,30 @@
 
 
 def late_kernel(first, *refs):
-    parts, w, out = refs[:-2], refs[-2], refs[-1]
+    parts, (w, out, done, sems) = refs[:-4], refs[-4:]
     width = parts[0].shape[1]
-    total = first[...]
-    for k, part in enumerate(parts):
-        total = total + dot_nn(part[...], w[(k + 1) * width : (k + 2) * width, :])
-    out[...] = total.astype(BF16)
-
-
-def call(body, outs, specs, args, limit, scratch=()):
+    pieces = sems.shape[0]
+    size = out.shape[1] // pieces
+    copies = []
+    for i in range(pieces):
+        cols = slice(i * size, (i + 1) * size)
+        total = first[:, cols]
+        for k, part in enumerate(parts):
+            total = total + dot_nn(part[...], w[(k + 1) * width : (k + 2) * width, cols])
+        done[:, cols] = total.astype(BF16)
+        copies.append(pltpu.make_async_copy(done.at[:, cols], out.at[:, cols], sems.at[i]))
+        copies[-1].start()
+    for copy in copies:
+        copy.wait()
+
+
+def call(body, outs, specs, args, limit, scratch=(), out_spec=VM):
     shapes = tuple(jax.ShapeDtypeStruct(shape, dtype) for shape, dtype in outs)
     result = pl.pallas_call(
         body,
         out_shape=shapes,
         in_specs=specs,
-        out_specs=(VM,) * len(shapes),
+        out_specs=(out_spec,) * len(shapes),
         scratch_shapes=list(scratch),
         compiler_params=pltpu.CompilerParams(vmem_limit_bytes=limit),
         cost_estimate=pl.CostEstimate(flops=0, bytes_accessed=0, transcendentals=0),
@@ -411,7 +420,7 @@
         phi_kernel, [((heads, rows, count), BF16)], [VM] * 3, (kv, both, factors), limit
     )
     sent = keep.astype(BF16)
-    first, second, third = [crossed(sent, bit) for bit in (6, 2, 4)]
+    first, second, third = [crossed(sent, bit) for bit in (2, 6, 4)]
     first, second, third, kv, phi_q = lax.optimization_barrier((first, second, third, kv, phi_q))
     keep = keep + first.astype(F32) + second.astype(F32) + third.astype(F32)
     far_rest = gathered(far_own)
@@ -465,6 +474,8 @@
         [VM] * (1 + groups),
         (first, *returned, w_out),
         limit,
+        scratch=[pltpu.VMEM((mine, w_out.shape[1]), BF16), pltpu.SemaphoreType.DMA((4,))],
+        out_spec=HB,
     )
 
 

time: 30.8 us -> 32.4 us (1.052)
  waiting for transfers between devices: 5.95 us -> 8.53 us
  starting transfers between devices: 13.8 us -> 12.8 us
    ppermute x7, waiting for transfers between devices: 1.7 us -> 4.26 us  [crossed(): return lax.ppermute(array, 'dom', [(i, i ^ bit) for i in range(doms)])]
    ppermute x7, starting transfers between devices: 5.93 us -> 5.03 us  [crossed(): return lax.ppermute(array, 'dom', [(i, i ^ bit) for i in range(doms)])]
  transfers between devices with their start and end apart: 11 -> 11, of which waited for: 5 -> 8; matrix products, arithmetic and copies ran while one was open for 0% -> 0% of each run, Pallas kernels for 31% -> 29%
where the time goes in v4:
time: 32.4 us; the launch traced here: 32.3 us
  starting transfers between devices  12.8 us (40%)
  Pallas kernels  10.6 us (33%)
  waiting for transfers between devices  8.53 us (26%)
    pallas_call x13, Pallas kernels, call(): pl.pallas_call(body, out_shape=shapes, in_specs=specs, out_specs=(out_spe...  10.6 us
    ppermute x7, starting transfers between devices, crossed(): return lax.ppermute(array, 'dom', [(i, i ^ bit) for i in range(doms)])  5.03 us
    ppermute x3, waiting for transfers between devices, shifted(): lax.ppermute(array, 'head', [(i, (i + step) % groups) for i in range(grou...  4.27 us
    ppermute x7, waiting for transfers between devices, crossed(): return lax.ppermute(array, 'dom', [(i, i ^ bit) for i in range(doms)])  4.26 us
    ppermute x3, starting transfers between devices, shifted(): lax.ppermute(array, 'head', [(i, (i + step) % groups) for i in range(grou...  4.05 us
    ppermute x1, starting transfers between devices, shards(): lax.ppermute(node_feats, 'dom', pairs + [(b, a) for a, b in pairs])  3.69 us
  transfers between devices with their start and end apart: 11, of which 8 were waited for; matrix products, arithmetic and copies ran while one was open for 0% of the time, Pallas kernels for 29%

profile of v4, /device:TPU:0, one launch (start us, length us, event | category | flops | bytes accessed | tf_op | source)
XLA Modules:
  0.0 32.3 jit_solution(1037547077585698261)
XLA Ops:
  0.0 3.0 %collective-permute-start = (bf16[128,512]{1,0:T(8,128)(2,1)}, bf16[128,512]{1,0:T(8,128)(2,1)S(1)}, u32[]{:S(2)}, u32[]{:S(2)}) collective-permute-start(bf16[128,512]{1,0:T(8,128)(2,1)} %own.1), channel_id=1, source_target_pairs={{0,1},{1,0},{2,3},{3,2},{4,5},{5,4},{6,7},{7,6},{8,9},{9,8},{10,11... | collective-permute-start | bytes 393224 | tf_op jit(solution)/shard_map/ppermute | solution.py:327
  3.0 3.7 %collective-permute-start.2 = (bf16[128,512]{1,0:T(8,128)(2,1)}, bf16[128,512]{1,0:T(8,128)(2,1)S(1)}, u32[]{:S(2)}, u32[]{:S(2)}) collective-permute-start(bf16[128,512]{1,0:T(8,128)(2,1)} %own.1), channel_id=1, source_target_pairs={{2,4},{6,8},{10,12},{14,16},{18,20},{22,24},{26,28},{30,0},{4,2},{... | collective-permute-start | bytes 393224 | tf_op jit(solution)/shard_map/ppermute | solution.py:373
  6.7 3.2 %shard_map.91 = (bf16[128,768]{1,0:T(8,128)(2,1)S(1)}, f32[264,256]{1,0:T(8,128)S(1)}, f32[1,512]{1,0:T(1,128)S(1)}, bf16[512,768]{1,0:T(8,128)(2,1)S(1)}, bf16[...) custom-call(s32[2]{0:T(128)S(1)} %pad_add_fusion.where, ...), custom_call_target="tpu_custom_call" | custom-call | tf_op jit(solution)/shard_map/pallas_call | solution.py:300
  9.9 0.4 %shard_map.92 = (bf16[128,768]{1,0:T(8,128)(2,1)S(1)}, bf16[256,512]{1,0:T(8,128)(2,1)S(1)}) custom-call(bf16[128,512]{1,0:T(8,128)(2,1)S(1)} %collective-permute-done.feats, bf16[128,512]{1,0:T(8,128)(2,1)S(1)} %copy-done, f32[1,512]{1,0:T(1,128)S(1)} %get-tuple-element.30.gain, bf16[512,768]{1,0:T(8,128)(2,1)S(1)} %get-tuple-element.31.w), custom_call_target="tpu_custom_call" | custom-call | tf_op jit(solution)/shard_map/pallas_call | solution.py:300
  10.4 0.6 %shard_map.94 = bf16[136,256]{1,0:T(8,128)(2,1)S(1)} custom-call(bf16[128,768]{1,0:T(8,128)(2,1)S(1)} %get-tuple-element.32.qkv.rest, bf16[4,128,256]{2,1,0:T(8,128)(2,1)S(1)} %get-tuple-element.33.both, f32[4,1]{1,0:T(4,128)S(1)} %get-tuple-element.34.factors, f32[128,1]{1,0:T(8,128)S(1)} %get-tuple-element.35.hidden, f32[264,256]{1,0:T(8,128)S(1)} %get-tuple-element.36.sums), custom_call_target="tpu_custom_call" | custom-call | tf_op jit(solution)/shard_map/pallas_call | solution.py:300
  11.0 0.6 %shard_map.93 = f32[136,256]{1,0:T(8,128)S(1)} custom-call(bf16[128,768]{1,0:T(8,128)(2,1)S(1)} %get-tuple-element.32.qkv.rest, bf16[4,128,256]{2,1,0:T(8,128)(2,1)S(1)} %get-tuple-element.33.both, f32[4,1]{1,0:T(4,128)S(1)} %get-tuple-element.34.factors, f32[128,1]{1,0:T(8,128)S(1)} %get-tuple-element.35.hidden, f32[264,256]{1,0:T(8,128)S(1)} %get-tuple-element.36.sums), custom_call_target="tpu_custom_call" | custom-call | tf_op jit(solution)/shard_map/pallas_call | solution.py:300
  11.6 0.6 %collective-permute-start.6 = (bf16[256,512]{1,0:T(8,128)(2,1)S(1)}, bf16[256,512]{1,0:T(8,128)(2,1)S(1)}, u32[]{:S(2)}, u32[]{:S(2)}) collective-permute-start(bf16[256,512]{1,0:T(8,128)(2,1)S(1)} %get-tuple-element.38), channel_id=1, source_target_pairs={{0,2},{2,0},{4,6},{6,4},{8,10},{10,8},{12,14},{14,12},{16,18},{18,... | collective-permute-start | bytes 786440 | tf_op jit(solution)/shard_map/ppermute | solution.py:334
  12.4 0.6 %collective-permute-start.4 = (bf16[136,256]{1,0:T(8,128)(2,1)S(1)}, bf16[136,256]{1,0:T(8,128)(2,1)S(1)}, u32[]{:S(2)}, u32[]{:S(2)}) collective-permute-start(bf16[136,256]{1,0:T(8,128)(2,1)S(1)} %fusion), channel_id=1, source_target_pairs={{0,12},{2,14},{4,8},{6,10},{8,4},{10,6},{12,0},{14,2},{16,28},{18,... | collective-permute-start | bytes 208904 | tf_op jit(solution)/shard_map/ppermute | solution.py:334
  13.0 2.9 %collective-permute-start.5 = (bf16[136,256]{1,0:T(8,128)(2,1)S(1)}, bf16[136,256]{1,0:T(8,128)(2,1)S(1)}, u32[]{:S(2)}, u32[]{:S(2)}) collective-permute-start(bf16[136,256]{1,0:T(8,128)(2,1)S(1)} %fusion), channel_id=1, source_target_pairs={{0,8},{2,10},{4,12},{6,14},{8,0},{10,2},{12,4},{14,6},{16,24},{18,... | collective-permute-start | bytes 208904 | tf_op jit(solution)/shard_map/ppermute | solution.py:334
  15.9 0.5 %collective-permute-start.8 = (bf16[128,512]{1,0:T(8,128)(2,1)S(1)}, bf16[128,512]{1,0:T(8,128)(2,1)S(1)}, u32[]{:S(2)}, u32[]{:S(2)}) collective-permute-start(bf16[128,512]{1,0:T(8,128)(2,1)S(1)} %collective-permute-done.2.far_own), channel_id=1, source_target_pairs={{0,1},{1,0},{2,3},{3,2},{4,5},{5,4},{6,7},{7,6},{8,9},{9,8},{10,11... | collective-permute-start | bytes 393224 | tf_op jit(solution)/shard_map/ppermute | solution.py:327
  16.4 0.6 %shard_map.95.kv = bf16[512,768]{1,0:T(8,128)(2,1)S(1)} custom-call(bf16[256,512]{1,0:T(8,128)(2,1)S(1)} %collective-permute-done.6.near, f32[1,512]{1,0:T(1,128)S(1)} %get-tuple-element.30.gain, bf16[512,768]{1,0:T(8,128)(2,1)S(1)} %get-tuple-element.31.w, bf16[128,768]{1,0:T(8,128)(2,1)S(1)} %get-tuple-element.39.own, ...), custom_call_target="tpu_custom_call" | custom-call | tf_op jit(solution)/shard_map/pallas_call | solution.py:300
  17.0 0.6 %shard_map.96.phi_q = bf16[4,256,256]{2,1,0:T(8,128)(2,1)S(1)} custom-call(bf16[512,768]{1,0:T(8,128)(2,1)S(1)} %shard_map.95.kv, bf16[4,128,256]{2,1,0:T(8,128)(2,1)S(1)} %get-tuple-element.33.both, f32[4,1]{1,0:T(4,128)S(1)} %get-tuple-element.34.factors), custom_call_target="tpu_custom_call" | custom-call | tf_op jit(solution)/shard_map/pallas_call | solution.py:300
  18.0 0.4 %collective-permute-done.4 = bf16[136,256]{1,0:T(8,128)(2,1)S(1)} collective-permute-done((bf16[136,256]{1,0:T(8,128)(2,1)S(1)}, bf16[136,256]{1,0:T(8,128)(2,1)S(1)}, u32[]{:S(2)}, u32[]{:S(2)}) %collective-permute-start.4) | collective-permute-done | bytes 69664 | tf_op jit(solution)/shard_map/ppermute | solution.py:334
  18.3 1.0 %collective-permute-done.5 = bf16[136,256]{1,0:T(8,128)(2,1)S(1)} collective-permute-done((bf16[136,256]{1,0:T(8,128)(2,1)S(1)}, bf16[136,256]{1,0:T(8,128)(2,1)S(1)}, u32[]{:S(2)}, u32[]{:S(2)}) %collective-permute-start.5) | collective-permute-done | bytes 69664 | tf_op jit(solution)/shard_map/ppermute | solution.py:334
  19.3 0.8 %collective-permute-start.7 = (bf16[136,256]{1,0:T(8,128)(2,1)S(1)}, bf16[136,256]{1,0:T(8,128)(2,1)S(1)}, u32[]{:S(2)}, u32[]{:S(2)}) collective-permute-start(bf16[136,256]{1,0:T(8,128)(2,1)S(1)} %fusion.1), channel_id=1, source_target_pairs={{0,16},{2,18},{4,20},{6,22},{8,24},{10,26},{12,28},{14,30},{16,0},... | collective-permute-start | bytes 208904 | tf_op jit(solution)/shard_map/ppermute | solution.py:334
  20.1 0.7 %collective-permute-done.8.far_rest = bf16[128,512]{1,0:T(8,128)(2,1)S(1)} collective-permute-done((bf16[128,512]{1,0:T(8,128)(2,1)S(1)}, bf16[128,512]{1,0:T(8,128)(2,1)S(1)}, u32[]{:S(2)}, u32[]{:S(2)}) %collective-permute-start.8) | collective-permute-done | bytes 131104 | tf_op jit(solution)/shard_map/ppermute | solution.py:327
  20.8 0.6 %shard_map.97.far = bf16[256,768]{1,0:T(8,128)(2,1)S(1)} custom-call(bf16[128,512]{1,0:T(8,128)(2,1)S(1)} %collective-permute-done.2.far_own, bf16[128,512]{1,0:T(8,128)(2,1)S(1)} %collective-permute-done.8.far_rest, f32[1,512]{1,0:T(1,128)S(1)} %get-tuple-element.30.gain, bf16[512,768]{1,0:T(8,128)(2,1)S(1)} %get-tuple-element.31.w), custom_call_target="tpu_custom_call" | custom-call | tf_op jit(solution)/shard_map/pallas_call | solution.py:300
  21.4 1.2 %shard_map.98.local = f32[256,128]{1,0:T(8,128)S(1)} custom-call(bf16[512,768]{1,0:T(8,128)(2,1)S(1)} %shard_map.95.kv, bf16[256,768]{1,0:T(8,128)(2,1)S(1)} %shard_map.97.far, f32[2,768]{1,0:T(2,128)S(1)} %get-tuple-element.46.bias), custom_call_target="tpu_custom_call" | custom-call | tf_op jit(solution)/shard_map/pallas_call | solution.py:300
  22.6 1.2 %shard_map.99.local = f32[256,128]{1,0:T(8,128)S(1)} custom-call(bf16[512,768]{1,0:T(8,128)(2,1)S(1)} %shard_map.95.kv, bf16[256,768]{1,0:T(8,128)(2,1)S(1)} %shard_map.97.far, f32[2,768]{1,0:T(2,128)S(1)} %get-tuple-element.46.bias), custom_call_target="tpu_custom_call" | custom-call | tf_op jit(solution)/shard_map/pallas_call | solution.py:300
  23.8 1.5 %collective-permute-done.7 = bf16[136,256]{1,0:T(8,128)(2,1)S(1)} collective-permute-done((bf16[136,256]{1,0:T(8,128)(2,1)S(1)}, bf16[136,256]{1,0:T(8,128)(2,1)S(1)}, u32[]{:S(2)}, u32[]{:S(2)}) %collective-permute-start.7) | collective-permute-done | bytes 69664 | tf_op jit(solution)/shard_map/ppermute | solution.py:334
  25.8 0.9 %collective-permute-done.9.sums = bf16[136,256]{1,0:T(8,128)(2,1)S(1)} collective-permute-done((bf16[136,256]{1,0:T(8,128)(2,1)S(1)}, bf16[136,256]{1,0:T(8,128)(2,1)S(1)}, u32[]{:S(2)}, u32[]{:S(2)}) %collective-permute-start.9) | collective-permute-done | bytes 69664 | tf_op jit(solution)/shard_map/ppermute | solution.py:334
  27.0 0.6 %collective-permute-start.10 = (bf16[128,256]{1,0:T(8,128)(2,1)S(1)}, bf16[128,256]{1,0:T(8,128)(2,1)S(1)}, u32[]{:S(2)}, u32[]{:S(2)}) collective-permute-start(bf16[128,256]{1,0:T(8,128)(2,1)S(1)} %bitcast.4), channel_id=1, source_target_pairs={{0,1},{1,0},{2,3},{3,2},{4,5},{5,4},{6,7},{7,6},{8,9},{9,8},{10,11... | collective-permute-start | bytes 196616 | tf_op jit(solution)/shard_map/ppermute | solution.py:327
  27.8 3.6 %collective-permute-done.10.refs_0_ = bf16[128,256]{1,0:T(8,128)(2,1)S(1)} collective-permute-done((bf16[128,256]{1,0:T(8,128)(2,1)S(1)}, bf16[128,256]{1,0:T(8,128)(2,1)S(1)}, u32[]{:S(2)}, u32[]{:S(2)}) %collective-permute-start.10) | collective-permute-done | bytes 65568 | tf_op jit(solution)/shard_map/ppermute | solution.py:327
  31.4 0.9 %shard_map.103 = bf16[128,512]{1,0:T(8,128)(2,1)} custom-call(f32[128,512]{1,0:T(8,128)S(1)} %shard_map.102.first, bf16[128,256]{1,0:T(8,128)(2,1)S(1)} %collective-permute-done.10.refs_0_, bf16[512,512]{1,0:T(8,128)(2,1)S(1)} %get-tuple-element.53.w.refs_1_), custom_call_target="tpu_custom_call" | custom-call | tf_op jit(solution)/shard_map/pallas_call | solution.py:300
  (17 shorter events, 1.6 us)
Async XLA Ops:
  0.0 9.9 %collective-permute-start = (bf16[128,512]{1,0:T(8,128)(2,1)}, bf16[128,512]{1,0:T(8,128)(2,1)S(1)}, u32[]{:S(2)}, u32[]{:S(2)}) collective-permute-start(bf16[128,512]{1,0:T(8,128)(2,1)} %own.1), channel_id=1, source_target_pairs={{0,1},{1,0},{2,3},{3,2},{4,5},{5,4},{6,7},{7,6},{8,9},{9,8},{10,11... | collective-permute-start | bytes 393224 | tf_op jit(solution)/shard_map/ppermute | solution.py:327
  3.0 9.2 %collective-permute-start.2 = (bf16[128,512]{1,0:T(8,128)(2,1)}, bf16[128,512]{1,0:T(8,128)(2,1)S(1)}, u32[]{:S(2)}, u32[]{:S(2)}) collective-permute-start(bf16[128,512]{1,0:T(8,128)(2,1)} %own.1), channel_id=1, source_target_pairs={{2,4},{6,8},{10,12},{14,16},{18,20},{22,24},{26,28},{30,0},{4,2},{... | collective-permute-start | bytes 393224 | tf_op jit(solution)/shard_map/ppermute | solution.py:373
  6.7 3.2 %copy-start = (bf16[128,512]{1,0:T(8,128)(2,1)S(1)}, bf16[128,512]{1,0:T(8,128)(2,1)}, u32[]{:S(2)}) copy-start(bf16[128,512]{1,0:T(8,128)(2,1)} %own.1) | copy-start | bytes 393220
  11.0 1.3 %collective-permute-start.1 = (bf16[136,256]{1,0:T(8,128)(2,1)S(1)}, bf16[136,256]{1,0:T(8,128)(2,1)S(1)}, u32[]{:S(2)}, u32[]{:S(2)}) collective-permute-start(bf16[136,256]{1,0:T(8,128)(2,1)S(1)} %shard_map.94), channel_id=1, source_target_pairs={{0,2},{2,0},{4,6},{6,4},{8,10},{10,8},{12,14},{14,12},{16,18},{18,... | collective-permute-start | bytes 208904 | tf_op jit(solution)/shard_map/ppermute | solution.py:334
  11.6 4.8 %collective-permute-start.6 = (bf16[256,512]{1,0:T(8,128)(2,1)S(1)}, bf16[256,512]{1,0:T(8,128)(2,1)S(1)}, u32[]{:S(2)}, u32[]{:S(2)}) collective-permute-start(bf16[256,512]{1,0:T(8,128)(2,1)S(1)} %get-tuple-element.38), channel_id=1, source_target_pairs={{0,2},{2,0},{4,6},{6,4},{8,10},{10,8},{12,14},{14,12},{16,18},{18,... | collective-permute-start | bytes 786440 | tf_op jit(solution)/shard_map/ppermute | solution.py:334
  12.3 5.7 %collective-permute-start.3 = (bf16[136,256]{1,0:T(8,128)(2,1)S(1)}, bf16[136,256]{1,0:T(8,128)(2,1)S(1)}, u32[]{:S(2)}, u32[]{:S(2)}) collective-permute-start(bf16[136,256]{1,0:T(8,128)(2,1)S(1)} %fusion), channel_id=1, source_target_pairs={{0,4},{2,6},{4,0},{6,2},{8,12},{10,14},{12,8},{14,10},{16,20},{18,... | collective-permute-start | bytes 208904 | tf_op jit(solution)/shard_map/ppermute | solution.py:334
  12.4 6.0 %collective-permute-start.4 = (bf16[136,256]{1,0:T(8,128)(2,1)S(1)}, bf16[136,256]{1,0:T(8,128)(2,1)S(1)}, u32[]{:S(2)}, u32[]{:S(2)}) collective-permute-start(bf16[136,256]{1,0:T(8,128)(2,1)S(1)} %fusion), channel_id=1, source_target_pairs={{0,12},{2,14},{4,8},{6,10},{8,4},{10,6},{12,0},{14,2},{16,28},{18,... | collective-permute-start | bytes 208904 | tf_op jit(solution)/shard_map/ppermute | solution.py:334
  13.0 6.3 %collective-permute-start.5 = (bf16[136,256]{1,0:T(8,128)(2,1)S(1)}, bf16[136,256]{1,0:T(8,128)(2,1)S(1)}, u32[]{:S(2)}, u32[]{:S(2)}) collective-permute-start(bf16[136,256]{1,0:T(8,128)(2,1)S(1)} %fusion), channel_id=1, source_target_pairs={{0,8},{2,10},{4,12},{6,14},{8,0},{10,2},{12,4},{14,6},{16,24},{18,... | collective-permute-start | bytes 208904 | tf_op jit(solution)/shard_map/ppermute | solution.py:334
  15.9 5.0 %collective-permute-start.8 = (bf16[128,512]{1,0:T(8,128)(2,1)S(1)}, bf16[128,512]{1,0:T(8,128)(2,1)S(1)}, u32[]{:S(2)}, u32[]{:S(2)}) collective-permute-start(bf16[128,512]{1,0:T(8,128)(2,1)S(1)} %collective-permute-done.2.far_own), channel_id=1, source_target_pairs={{0,1},{1,0},{2,3},{3,2},{4,5},{5,4},{6,7},{7,6},{8,9},{9,8},{10,11... | collective-permute-start | bytes 393224 | tf_op jit(solution)/shard_map/ppermute | solution.py:327
  19.3 6.0 %collective-permute-start.7 = (bf16[136,256]{1,0:T(8,128)(2,1)S(1)}, bf16[136,256]{1,0:T(8,128)(2,1)S(1)}, u32[]{:S(2)}, u32[]{:S(2)}) collective-permute-start(bf16[136,256]{1,0:T(8,128)(2,1)S(1)} %fusion.1), channel_id=1, source_target_pairs={{0,16},{2,18},{4,20},{6,22},{8,24},{10,26},{12,28},{14,30},{16,0},... | collective-permute-start | bytes 208904 | tf_op jit(solution)/shard_map/ppermute | solution.py:334
  25.4 1.3 %collective-permute-start.9 = (bf16[136,256]{1,0:T(8,128)(2,1)S(1)}, bf16[136,256]{1,0:T(8,128)(2,1)S(1)}, u32[]{:S(2)}, u32[]{:S(2)}) collective-permute-start(bf16[136,256]{1,0:T(8,128)(2,1)S(1)} %add_convert_fusion.sums), channel_id=1, source_target_pairs={{0,2},{2,0},{4,6},{6,4},{8,10},{10,8},{12,14},{14,12},{16,18},{18,... | collective-permute-start | bytes 208904 | tf_op jit(solution)/shard_map/ppermute | solution.py:334
  27.0 4.3 %collective-permute-start.10 = (bf16[128,256]{1,0:T(8,128)(2,1)S(1)}, bf16[128,256]{1,0:T(8,128)(2,1)S(1)}, u32[]{:S(2)}, u32[]{:S(2)}) collective-permute-start(bf16[128,256]{1,0:T(8,128)(2,1)S(1)} %bitcast.4), channel_id=1, source_target_pairs={{0,1},{1,0},{2,3},{3,2},{4,5},{5,4},{6,7},{7,6},{8,9},{9,8},{10,11... | collective-permute-start | bytes 196616 | tf_op jit(solution)/shard_map/ppermute | solution.py:327

commit v5 on v3

--- a/solution.py
+++ b/solution.py
@@ -79,7 +79,7 @@
 
 def own_kernel(
     heads, groups, where, temper_in, fill_in, src_in, used_in, feats_in, gain_in, w_in,
-    directions_in, w_out_in, qkv, sums, gain, w, both, w_out, factors, hidden, bias, feats,
+    directions_in, w_out_in, qkv, own_hidden, gain, w, both, w_out, factors, hidden, bias, feats,
     directions, temper, fill, src, used, sems
 ):
     width = w_out.shape[0] // groups
@@ -137,18 +137,11 @@
         for t in range(mine)
     ]
     hidden[...] = hide(fills[mine:])
-    own_hidden = hide(fills[:mine])
-    totals = []
+    own_hidden[...] = hide(fills[:mine])
     for h in range(heads):
         scale = row_scale(temper[head_at(heads, where, h)], head_dim)
         factors[h : h + 1] = scale * scale * (0.5 * LOG2E)
         both[h] = split_directions(directions[h], scale)
-    for h in range(heads):
-        part, total = head_sums(h, out, both, factors[h : h + 1], own_hidden)
-        sums[h * head_dim : (h + 1) * head_dim] = part
-        totals.append(total)
-    totals.append(jnp.zeros((EXTRA - heads, count), F32))
-    sums[heads * head_dim :] = jnp.concatenate(totals, axis=0)
     write_bias(groups, mine, where, src, used, fill, bias)
     for item in on_out:
         item.wait()
@@ -177,15 +170,14 @@
                 bias[i : i + 1, cols] = jnp.where(lane < real, jnp.log(level) * LOG2E, NEG)
 
 
-def bundle(chosen, out, both, factors, hidden, sums):
+def bundle(chosen, out, both, factors, hidden):
     head_dim = both.shape[1] // 2
-    inner = sums.shape[0] - EXTRA
     parts, totals = [], []
     for h in chosen:
         part, total = head_sums(h, out, both, factors[h : h + 1], hidden[...])
-        parts.append(part + sums[h * head_dim : (h + 1) * head_dim])
-        totals.append(total + sums[inner + h : inner + h + 1])
-    spare = jnp.zeros((EXTRA - len(totals), sums.shape[1]), F32)
+        parts.append(part)
+        totals.append(total)
+    spare = jnp.zeros((EXTRA - len(totals), both.shape[2]), F32)
     return jnp.concatenate(parts + totals + [spare], axis=0)
 
 
@@ -195,8 +187,12 @@
     pair[own.shape[0] :] = feats[...]
 
 
-def sums_kernel(chosen, qkv, both, factors, hidden, sums, out):
-    out[...] = bundle(chosen, qkv, both, factors, hidden, sums).astype(out.dtype)
+def sums_kernel(chosen, qkv, both, factors, hidden, *refs):
+    *before, out = refs
+    total = bundle(chosen, qkv, both, factors, hidden)
+    if before:
+        total = total + before[0][...]
+    out[...] = total.astype(out.dtype)
 
 
 def near_kernel(near, gain, w, own, rest, kv):
@@ -331,11 +327,11 @@
     turns = 2 if heads % 2 == 0 else 1
     if heads == 1:
         temper = jnp.concatenate([temper, temper])
-    qkv_own, sums, gain, w_qkv, both, w_out, factors, hidden, bias = call(
+    qkv_own, own_hidden, gain, w_qkv, both, w_out, factors, hidden, bias = call(
         functools.partial(own_kernel, heads, groups),
         [
             ((mine, cols), BF16),
-            ((inner + EXTRA, count), F32),
+            ((mine, 1), F32),
             ((1, width), F32),
             ((width, cols), BF16),
             ((heads, 2 * head_dim, count), BF16),
@@ -371,11 +367,18 @@
     )
 
     def summed(chosen, dtype):
+        own = call(
+            functools.partial(sums_kernel, chosen),
+            [((len(chosen) * head_dim + EXTRA, count), F32)],
+            [VM] * 4,
+            (qkv_own, both, factors, own_hidden),
+            limit,
+        )
         return call(
             functools.partial(sums_kernel, chosen),
             [((len(chosen) * head_dim + EXTRA, count), dtype)],
             [VM] * 5,
-            (qkv_rest, both, factors, hidden, sums),
+            (qkv_rest, both, factors, hidden, own),
             limit,
         )
 

time: 30.8 us -> 31.4 us (1.019)
  local copies, waits for them, and re-layouts: 0.01 us -> 0.33 us
    pallas_call x13 -> x15, Pallas kernels: 10.6 us -> 10.9 us  [call(): pl.pallas_call(body, out_shape=shapes, in_specs=specs, out_specs=(VM,) *...]
    unnamed x2, local copies, waits for them, and re-layouts: 0.01 us -> 0.33 us
  transfers between devices with their start and end apart: 11 -> 11, of which waited for: 5 -> 4; matrix products, arithmetic and copies ran while one was open for 0% -> 0% of each run, Pallas kernels for 31% -> 31%
where the time goes in v5:
time: 31.4 us; the launch traced here: 31.3 us
  starting transfers between devices  13.8 us (44%)
  Pallas kernels  10.9 us (35%)
  waiting for transfers between devices  5.84 us (19%)
  local copies, waits for them, and re-layouts  0.33 us (1%)
    pallas_call x15, Pallas kernels, call(): pl.pallas_call(body, out_shape=shapes, in_specs=specs, out_specs=(VM,) *...  10.9 us
    ppermute x7, starting transfers between devices, crossed(): return lax.ppermute(array, 'dom', [(i, i ^ bit) for i in range(doms)])  5.9 us
    ppermute x3, waiting for transfers between devices, shifted(): lax.ppermute(array, 'head', [(i, (i + step) % groups) for i in range(grou...  4.37 us
    ppermute x3, starting transfers between devices, shifted(): lax.ppermute(array, 'head', [(i, (i + step) % groups) for i in range(grou...  4.21 us
    ppermute x1, starting transfers between devices, shards(): lax.ppermute(node_feats, 'dom', pairs + [(b, a) for a, b in pairs])  3.69 us
    ppermute x7, waiting for transfers between devices, crossed(): return lax.ppermute(array, 'dom', [(i, i ^ bit) for i in range(doms)])  1.47 us
  transfers between devices with their start and end apart: 11, of which 4 were waited for; matrix products, arithmetic and copies ran while one was open for 0% of the time, Pallas kernels for 31%

profile of v5, /device:TPU:0, one launch (start us, length us, event | category | flops | bytes accessed | tf_op | source)
XLA Modules:
  0.0 31.3 jit_solution(18195870526780835954)
XLA Ops:
  0.0 3.0 %collective-permute-start = (bf16[128,512]{1,0:T(8,128)(2,1)}, bf16[128,512]{1,0:T(8,128)(2,1)S(1)}, u32[]{:S(2)}, u32[]{:S(2)}) collective-permute-start(bf16[128,512]{1,0:T(8,128)(2,1)} %own.1), channel_id=1, source_target_pairs={{0,1},{1,0},{2,3},{3,2},{4,5},{5,4},{6,7},{7,6},{8,9},{9,8},{10,11... | collective-permute-start | bytes 393224 | tf_op jit(solution)/shard_map/ppermute | solution.py:314
  3.0 3.7 %collective-permute-start.2 = (bf16[128,512]{1,0:T(8,128)(2,1)}, bf16[128,512]{1,0:T(8,128)(2,1)S(1)}, u32[]{:S(2)}, u32[]{:S(2)}) collective-permute-start(bf16[128,512]{1,0:T(8,128)(2,1)} %own.1), channel_id=1, source_target_pairs={{2,4},{6,8},{10,12},{14,16},{18,20},{22,24},{26,28},{30,0},{4,2},{... | collective-permute-start | bytes 393224 | tf_op jit(solution)/shard_map/ppermute | solution.py:360
  6.7 2.4 %shard_map.91 = (bf16[128,768]{1,0:T(8,128)(2,1)S(1)}, f32[128,1]{1,0:T(8,128)S(1)}, f32[1,512]{1,0:T(1,128)S(1)}, bf16[512,768]{1,0:T(8,128)(2,1)S(1)}, bf16[4,...) custom-call(s32[2]{0:T(128)S(1)} %pad_add_fusion.where, ...), custom_call_target="tpu_custom_call" | custom-call | tf_op jit(solution)/shard_map/pallas_call | solution.py:287
  9.2 0.6 %shard_map.95.refs_0_ = f32[136,256]{1,0:T(8,128)S(1)} custom-call(bf16[128,768]{1,0:T(8,128)(2,1)S(1)} %get-tuple-element.36.qkv.own, bf16[4,128,256]{2,1,0:T(8,128)(2,1)S(1)} %get-tuple-element.33.both, f32[4,1]{1,0:T(4,128)S(1)} %get-tuple-element.34.factors, f32[128,1]{1,0:T(8,128)S(1)} %get-tuple-element.37.hidden), custom_call_target="tpu_custom_call" | custom-call | tf_op jit(solution)/shard_map/pallas_call | solution.py:287
  10.1 0.4 %shard_map.92 = (bf16[128,768]{1,0:T(8,128)(2,1)S(1)}, bf16[256,512]{1,0:T(8,128)(2,1)S(1)}) custom-call(bf16[128,512]{1,0:T(8,128)(2,1)S(1)} %collective-permute-done.feats, bf16[128,512]{1,0:T(8,128)(2,1)S(1)} %copy-done, f32[1,512]{1,0:T(1,128)S(1)} %get-tuple-element.30.gain, bf16[512,768]{1,0:T(8,128)(2,1)S(1)} %get-tuple-element.31.w), custom_call_target="tpu_custom_call" | custom-call | tf_op jit(solution)/shard_map/pallas_call | solution.py:287
  10.5 0.6 %shard_map.96 = bf16[136,256]{1,0:T(8,128)(2,1)S(1)} custom-call(bf16[128,768]{1,0:T(8,128)(2,1)S(1)} %get-tuple-element.32.qkv.rest, bf16[4,128,256]{2,1,0:T(8,128)(2,1)S(1)} %get-tuple-element.33.both, f32[4,1]{1,0:T(4,128)S(1)} %get-tuple-element.34.factors, f32[128,1]{1,0:T(8,128)S(1)} %get-tuple-element.35.hidden, f32[136,256]{1,0:T(8,128)S(1)} %shard_map.95.refs_0_), custom_call_target="tpu_custom_call" | custom-call | tf_op jit(solution)/shard_map/pallas_call | solution.py:287
  11.2 0.6 %shard_map.93.refs_0_ = f32[136,256]{1,0:T(8,128)S(1)} custom-call(bf16[128,768]{1,0:T(8,128)(2,1)S(1)} %get-tuple-element.36.qkv.own, bf16[4,128,256]{2,1,0:T(8,128)(2,1)S(1)} %get-tuple-element.33.both, f32[4,1]{1,0:T(4,128)S(1)} %get-tuple-element.34.factors, f32[128,1]{1,0:T(8,128)S(1)} %get-tuple-element.37.hidden), custom_call_target="tpu_custom_call" | custom-call | tf_op jit(solution)/shard_map/pallas_call | solution.py:287
  11.7 0.6 %collective-permute-start.6 = (bf16[256,512]{1,0:T(8,128)(2,1)S(1)}, bf16[256,512]{1,0:T(8,128)(2,1)S(1)}, u32[]{:S(2)}, u32[]{:S(2)}) collective-permute-start(bf16[256,512]{1,0:T(8,128)(2,1)S(1)} %get-tuple-element.39), channel_id=1, source_target_pairs={{0,2},{2,0},{4,6},{6,4},{8,10},{10,8},{12,14},{14,12},{16,18},{18,... | collective-permute-start | bytes 786440 | tf_op jit(solution)/shard_map/ppermute | solution.py:321
  12.3 0.6 %shard_map.94 = f32[136,256]{1,0:T(8,128)S(1)} custom-call(bf16[128,768]{1,0:T(8,128)(2,1)S(1)} %get-tuple-element.32.qkv.rest, bf16[4,128,256]{2,1,0:T(8,128)(2,1)S(1)} %get-tuple-element.33.both, f32[4,1]{1,0:T(4,128)S(1)} %get-tuple-element.34.factors, f32[128,1]{1,0:T(8,128)S(1)} %get-tuple-element.35.hidden, f32[136,256]{1,0:T(8,128)S(1)} %shard_map.93.refs_0_), custom_call_target="tpu_custom_call" | custom-call | tf_op jit(solution)/shard_map/pallas_call | solution.py:287
  13.0 0.4 %collective-permute-start.4 = (bf16[136,256]{1,0:T(8,128)(2,1)S(1)}, bf16[136,256]{1,0:T(8,128)(2,1)S(1)}, u32[]{:S(2)}, u32[]{:S(2)}) collective-permute-start(bf16[136,256]{1,0:T(8,128)(2,1)S(1)} %fusion), channel_id=1, source_target_pairs={{0,4},{2,6},{4,0},{6,2},{8,12},{10,14},{12,8},{14,10},{16,20},{18,... | collective-permute-start | bytes 208904 | tf_op jit(solution)/shard_map/ppermute | solution.py:321
  13.4 3.0 %collective-permute-start.5 = (bf16[136,256]{1,0:T(8,128)(2,1)S(1)}, bf16[136,256]{1,0:T(8,128)(2,1)S(1)}, u32[]{:S(2)}, u32[]{:S(2)}) collective-permute-start(bf16[136,256]{1,0:T(8,128)(2,1)S(1)} %fusion), channel_id=1, source_target_pairs={{0,8},{2,10},{4,12},{6,14},{8,0},{10,2},{12,4},{14,6},{16,24},{18,... | collective-permute-start | bytes 208904 | tf_op jit(solution)/shard_map/ppermute | solution.py:321
  16.4 0.5 %collective-permute-start.8 = (bf16[128,512]{1,0:T(8,128)(2,1)S(1)}, bf16[128,512]{1,0:T(8,128)(2,1)S(1)}, u32[]{:S(2)}, u32[]{:S(2)}) collective-permute-start(bf16[128,512]{1,0:T(8,128)(2,1)S(1)} %collective-permute-done.2.far_own), channel_id=1, source_target_pairs={{0,1},{1,0},{2,3},{3,2},{4,5},{5,4},{6,7},{7,6},{8,9},{9,8},{10,11... | collective-permute-start | bytes 393224 | tf_op jit(solution)/shard_map/ppermute | solution.py:314
  17.0 0.6 %shard_map.97.kv = bf16[512,768]{1,0:T(8,128)(2,1)S(1)} custom-call(bf16[256,512]{1,0:T(8,128)(2,1)S(1)} %collective-permute-done.6.near, f32[1,512]{1,0:T(1,128)S(1)} %get-tuple-element.30.gain, bf16[512,768]{1,0:T(8,128)(2,1)S(1)} %get-tuple-element.31.w, bf16[128,768]{1,0:T(8,128)(2,1)S(1)} %get-tuple-element.36.qkv.own, ...), custom_call_target="tpu_custom_call" | custom-call | tf_op jit(solution)/shard_map/pallas_call | solution.py:287
  17.6 0.6 %shard_map.98.phi_q = bf16[4,256,256]{2,1,0:T(8,128)(2,1)S(1)} custom-call(bf16[512,768]{1,0:T(8,128)(2,1)S(1)} %shard_map.97.kv, bf16[4,128,256]{2,1,0:T(8,128)(2,1)S(1)} %get-tuple-element.33.both, f32[4,1]{1,0:T(4,128)S(1)} %get-tuple-element.34.factors), custom_call_target="tpu_custom_call" | custom-call | tf_op jit(solution)/shard_map/pallas_call | solution.py:287
  18.2 0.5 %collective-permute-done.3 = bf16[136,256]{1,0:T(8,128)(2,1)S(1)} collective-permute-done((bf16[136,256]{1,0:T(8,128)(2,1)S(1)}, bf16[136,256]{1,0:T(8,128)(2,1)S(1)}, u32[]{:S(2)}, u32[]{:S(2)}) %collective-permute-start.3) | collective-permute-done | bytes 69664 | tf_op jit(solution)/shard_map/ppermute | solution.py:321
  18.8 1.7 %collective-permute-start.7 = (bf16[136,256]{1,0:T(8,128)(2,1)S(1)}, bf16[136,256]{1,0:T(8,128)(2,1)S(1)}, u32[]{:S(2)}, u32[]{:S(2)}) collective-permute-start(bf16[136,256]{1,0:T(8,128)(2,1)S(1)} %fusion.1), channel_id=1, source_target_pairs={{0,16},{2,18},{4,20},{6,22},{8,24},{10,26},{12,28},{14,30},{16,0},... | collective-permute-start | bytes 208904 | tf_op jit(solution)/shard_map/ppermute | solution.py:321
  20.5 1.0 %collective-permute-done.8.far_rest = bf16[128,512]{1,0:T(8,128)(2,1)S(1)} collective-permute-done((bf16[128,512]{1,0:T(8,128)(2,1)S(1)}, bf16[128,512]{1,0:T(8,128)(2,1)S(1)}, u32[]{:S(2)}, u32[]{:S(2)}) %collective-permute-start.8) | collective-permute-done | bytes 131104 | tf_op jit(solution)/shard_map/ppermute | solution.py:314
  21.4 0.6 %shard_map.99.far = bf16[256,768]{1,0:T(8,128)(2,1)S(1)} custom-call(bf16[128,512]{1,0:T(8,128)(2,1)S(1)} %collective-permute-done.2.far_own, bf16[128,512]{1,0:T(8,128)(2,1)S(1)} %collective-permute-done.8.far_rest, f32[1,512]{1,0:T(1,128)S(1)} %get-tuple-element.30.gain, bf16[512,768]{1,0:T(8,128)(2,1)S(1)} %get-tuple-element.31.w), custom_call_target="tpu_custom_call" | custom-call | tf_op jit(solution)/shard_map/pallas_call | solution.py:287
  22.0 1.2 %shard_map.101.local = f32[256,128]{1,0:T(8,128)S(1)} custom-call(bf16[512,768]{1,0:T(8,128)(2,1)S(1)} %shard_map.97.kv, bf16[256,768]{1,0:T(8,128)(2,1)S(1)} %shard_map.99.far, f32[2,768]{1,0:T(2,128)S(1)} %get-tuple-element.46.bias), custom_call_target="tpu_custom_call" | custom-call | tf_op jit(solution)/shard_map/pallas_call | solution.py:287
  23.2 1.2 %shard_map.100.local = f32[256,128]{1,0:T(8,128)S(1)} custom-call(bf16[512,768]{1,0:T(8,128)(2,1)S(1)} %shard_map.97.kv, bf16[256,768]{1,0:T(8,128)(2,1)S(1)} %shard_map.99.far, f32[2,768]{1,0:T(2,128)S(1)} %get-tuple-element.46.bias), custom_call_target="tpu_custom_call" | custom-call | tf_op jit(solution)/shard_map/pallas_call | solution.py:287
  24.9 0.9 %collective-permute-done.9.sums = bf16[136,256]{1,0:T(8,128)(2,1)S(1)} collective-permute-done((bf16[136,256]{1,0:T(8,128)(2,1)S(1)}, bf16[136,256]{1,0:T(8,128)(2,1)S(1)}, u32[]{:S(2)}, u32[]{:S(2)}) %collective-permute-start.9) | collective-permute-done | bytes 69664 | tf_op jit(solution)/shard_map/ppermute | solution.py:321
  26.1 0.7 %collective-permute-start.10 = (bf16[128,256]{1,0:T(8,128)(2,1)S(1)}, bf16[128,256]{1,0:T(8,128)(2,1)S(1)}, u32[]{:S(2)}, u32[]{:S(2)}) collective-permute-start(bf16[128,256]{1,0:T(8,128)(2,1)S(1)} %bitcast.4), channel_id=1, source_target_pairs={{0,1},{1,0},{2,3},{3,2},{4,5},{5,4},{6,7},{7,6},{8,9},{9,8},{10,11... | collective-permute-start | bytes 196616 | tf_op jit(solution)/shard_map/ppermute | solution.py:314
  27.0 3.4 %collective-permute-done.10.refs_0_ = bf16[128,256]{1,0:T(8,128)(2,1)S(1)} collective-permute-done((bf16[128,256]{1,0:T(8,128)(2,1)S(1)}, bf16[128,256]{1,0:T(8,128)(2,1)S(1)}, u32[]{:S(2)}, u32[]{:S(2)}) %collective-permute-start.10) | collective-permute-done | bytes 65568 | tf_op jit(solution)/shard_map/ppermute | solution.py:314
  30.5 0.8 %shard_map.105 = bf16[128,512]{1,0:T(8,128)(2,1)} custom-call(f32[128,512]{1,0:T(8,128)S(1)} %shard_map.104.first, bf16[128,256]{1,0:T(8,128)(2,1)S(1)} %collective-permute-done.10.refs_0_, bf16[512,512]{1,0:T(8,128)(2,1)S(1)} %get-tuple-element.53.w.refs_1_), custom_call_target="tpu_custom_call" | custom-call | tf_op jit(solution)/shard_map/pallas_call | solution.py:287
  (19 shorter events, 1.5 us)
Async XLA Ops:
  0.0 9.7 %collective-permute-start = (bf16[128,512]{1,0:T(8,128)(2,1)}, bf16[128,512]{1,0:T(8,128)(2,1)S(1)}, u32[]{:S(2)}, u32[]{:S(2)}) collective-permute-start(bf16[128,512]{1,0:T(8,128)(2,1)} %own.1), channel_id=1, source_target_pairs={{0,1},{1,0},{2,3},{3,2},{4,5},{5,4},{6,7},{7,6},{8,9},{9,8},{10,11... | collective-permute-start | bytes 393224 | tf_op jit(solution)/shard_map/ppermute | solution.py:314
  3.0 9.9 %collective-permute-start.2 = (bf16[128,512]{1,0:T(8,128)(2,1)}, bf16[128,512]{1,0:T(8,128)(2,1)S(1)}, u32[]{:S(2)}, u32[]{:S(2)}) collective-permute-start(bf16[128,512]{1,0:T(8,128)(2,1)} %own.1), channel_id=1, source_target_pairs={{2,4},{6,8},{10,12},{14,16},{18,20},{22,24},{26,28},{30,0},{4,2},{... | collective-permute-start | bytes 393224 | tf_op jit(solution)/shard_map/ppermute | solution.py:360
  9.2 0.9 %copy-start = (bf16[128,512]{1,0:T(8,128)(2,1)S(1)}, bf16[128,512]{1,0:T(8,128)(2,1)}, u32[]{:S(2)}) copy-start(bf16[128,512]{1,0:T(8,128)(2,1)} %own.1) | copy-start | bytes 393220
  11.1 1.8 %collective-permute-start.1 = (bf16[136,256]{1,0:T(8,128)(2,1)S(1)}, bf16[136,256]{1,0:T(8,128)(2,1)S(1)}, u32[]{:S(2)}, u32[]{:S(2)}) collective-permute-start(bf16[136,256]{1,0:T(8,128)(2,1)S(1)} %shard_map.96), channel_id=1, source_target_pairs={{0,2},{2,0},{4,6},{6,4},{8,10},{10,8},{12,14},{14,12},{16,18},{18,... | collective-permute-start | bytes 208904 | tf_op jit(solution)/shard_map/ppermute | solution.py:321
  11.7 5.2 %collective-permute-start.6 = (bf16[256,512]{1,0:T(8,128)(2,1)S(1)}, bf16[256,512]{1,0:T(8,128)(2,1)S(1)}, u32[]{:S(2)}, u32[]{:S(2)}) collective-permute-start(bf16[256,512]{1,0:T(8,128)(2,1)S(1)} %get-tuple-element.39), channel_id=1, source_target_pairs={{0,2},{2,0},{4,6},{6,4},{8,10},{10,8},{12,14},{14,12},{16,18},{18,... | collective-permute-start | bytes 786440 | tf_op jit(solution)/shard_map/ppermute | solution.py:321
  12.9 5.8 %collective-permute-start.3 = (bf16[136,256]{1,0:T(8,128)(2,1)S(1)}, bf16[136,256]{1,0:T(8,128)(2,1)S(1)}, u32[]{:S(2)}, u32[]{:S(2)}) collective-permute-start(bf16[136,256]{1,0:T(8,128)(2,1)S(1)} %fusion), channel_id=1, source_target_pairs={{0,12},{2,14},{4,8},{6,10},{8,4},{10,6},{12,0},{14,2},{16,28},{18,... | collective-permute-start | bytes 208904 | tf_op jit(solution)/shard_map/ppermute | solution.py:321
  13.0 5.8 %collective-permute-start.4 = (bf16[136,256]{1,0:T(8,128)(2,1)S(1)}, bf16[136,256]{1,0:T(8,128)(2,1)S(1)}, u32[]{:S(2)}, u32[]{:S(2)}) collective-permute-start(bf16[136,256]{1,0:T(8,128)(2,1)S(1)} %fusion), channel_id=1, source_target_pairs={{0,4},{2,6},{4,0},{6,2},{8,12},{10,14},{12,8},{14,10},{16,20},{18,... | collective-permute-start | bytes 208904 | tf_op jit(solution)/shard_map/ppermute | solution.py:321
  13.4 5.3 %collective-permute-start.5 = (bf16[136,256]{1,0:T(8,128)(2,1)S(1)}, bf16[136,256]{1,0:T(8,128)(2,1)S(1)}, u32[]{:S(2)}, u32[]{:S(2)}) collective-permute-start(bf16[136,256]{1,0:T(8,128)(2,1)S(1)} %fusion), channel_id=1, source_target_pairs={{0,8},{2,10},{4,12},{6,14},{8,0},{10,2},{12,4},{14,6},{16,24},{18,... | collective-permute-start | bytes 208904 | tf_op jit(solution)/shard_map/ppermute | solution.py:321
  16.4 5.0 %collective-permute-start.8 = (bf16[128,512]{1,0:T(8,128)(2,1)S(1)}, bf16[128,512]{1,0:T(8,128)(2,1)S(1)}, u32[]{:S(2)}, u32[]{:S(2)}) collective-permute-start(bf16[128,512]{1,0:T(8,128)(2,1)S(1)} %collective-permute-done.2.far_own), channel_id=1, source_target_pairs={{0,1},{1,0},{2,3},{3,2},{4,5},{5,4},{6,7},{7,6},{8,9},{9,8},{10,11... | collective-permute-start | bytes 393224 | tf_op jit(solution)/shard_map/ppermute | solution.py:314
  18.8 5.6 %collective-permute-start.7 = (bf16[136,256]{1,0:T(8,128)(2,1)S(1)}, bf16[136,256]{1,0:T(8,128)(2,1)S(1)}, u32[]{:S(2)}, u32[]{:S(2)}) collective-permute-start(bf16[136,256]{1,0:T(8,128)(2,1)S(1)} %fusion.1), channel_id=1, source_target_pairs={{0,16},{2,18},{4,20},{6,22},{8,24},{10,26},{12,28},{14,30},{16,0},... | collective-permute-start | bytes 208904 | tf_op jit(solution)/shard_map/ppermute | solution.py:321
  24.5 1.3 %collective-permute-start.9 = (bf16[136,256]{1,0:T(8,128)(2,1)S(1)}, bf16[136,256]{1,0:T(8,128)(2,1)S(1)}, u32[]{:S(2)}, u32[]{:S(2)}) collective-permute-start(bf16[136,256]{1,0:T(8,128)(2,1)S(1)} %add_convert_fusion.sums), channel_id=1, source_target_pairs={{0,2},{2,0},{4,6},{6,4},{8,10},{10,8},{12,14},{14,12},{16,18},{18,... | collective-permute-start | bytes 208904 | tf_op jit(solution)/shard_map/ppermute | solution.py:321
  26.1 4.3 %collective-permute-start.10 = (bf16[128,256]{1,0:T(8,128)(2,1)S(1)}, bf16[128,256]{1,0:T(8,128)(2,1)S(1)}, u32[]{:S(2)}, u32[]{:S(2)}) collective-permute-start(bf16[128,256]{1,0:T(8,128)(2,1)S(1)} %bitcast.4), channel_id=1, source_target_pairs={{0,1},{1,0},{2,3},{3,2},{4,5},{5,4},{6,7},{7,6},{8,9},{9,8},{10,11... | collective-permute-start | bytes 196616 | tf_op jit(solution)/shard_map/ppermute | solution.py:314
